TPU v7x, 128 devices: a whole 4x4x4 slice. The times are simulated.
128 devices in a mesh: row: 16 (over z, x), col: 8 (over y, core).
Axes of the slice: x: 4, y: 4, z: 4, core: 2. Of those that a mesh axis runs over, the one named last changes fastest.
Arguments:
- source: bfloat16 [65536, 128], P(('row', 'col')), may hold values from -1.5 to 1.5
- target: bfloat16 [32768, 128], P(('col', 'row')), may hold values from -1.5 to 1.5
Outputs:
- source_potential: float32 [65536], P('row')
- target_potential: float32 [32768], P('col')
All inputs are finite; a program needn't handle non-finite values.
Results may differ from a plain program's by a relative error of at most 0.0003.
Values may be sent and summed in bfloat16 or wider, within the bound.
A program may use at most 64 MiB of HBM per device.

v0:
```python
import jax
import jax.numpy as jnp
from jax import lax
from jax.sharding import PartitionSpec as P

ITERS = 3


entropic = 0.02


def pair_cost(source_block, source_sq_block, target_block, target_sq_block):
    inner = lax.dot_general(
        source_block, target_block, (((1,), (1,)), ((), ())), preferred_element_type=jnp.float32
    )
    return source_sq_block[:, None] + target_sq_block[None, :] - 2.0 * inner


def combine_pairs(first, second):
    highest = jnp.maximum(first[0], second[0])
    summed = first[1] * jnp.exp(first[0] - highest) + second[1] * jnp.exp(second[0] - highest)
    return (highest, summed)


def source_partials(source_rows, source_sq, target_rows, target_sq, target_pot):
    total_rows = source_rows.shape[0]
    total_cols = target_rows.shape[0]
    row_size = min(512, total_rows)
    row_count = total_rows // row_size
    col_size = min(1024, total_cols)

    def source_one_block(operands):
        block, block_sq = operands
        highest = jnp.full((row_size,), -jnp.inf, jnp.float32)
        summed = jnp.zeros((row_size,), jnp.float32)
        for offset in range(0, total_cols, col_size):
            scores = (
                target_pot[offset : offset + col_size][None, :]
                - pair_cost(
                    block,
                    block_sq,
                    target_rows[offset : offset + col_size],
                    target_sq[offset : offset + col_size],
                )
            ) / entropic
            block_high = jnp.max(scores, axis=1)
            block_sum = jnp.sum(jnp.exp(scores - block_high[:, None]), axis=1)
            highest, summed = combine_pairs((highest, summed), (block_high, block_sum))
        return (highest, summed)

    highest, summed = lax.map(
        source_one_block,
        (
            source_rows.reshape(row_count, row_size, source_rows.shape[1]),
            source_sq.reshape(row_count, row_size),
        ),
    )
    return (highest.reshape(total_rows), summed.reshape(total_rows))


def target_partials(source_rows, source_sq, target_rows, target_sq, source_pot):
    total_rows = source_rows.shape[0]
    total_cols = target_rows.shape[0]
    row_size = min(512, total_rows)
    row_count = total_rows // row_size
    col_size = min(1024, total_cols)

    def target_one_block(carried, operands):
        block, block_sq, block_pot = operands
        new_high = []
        new_sum = []
        for offset in range(0, total_cols, col_size):
            scores = (
                block_pot[:, None]
                - pair_cost(
                    block,
                    block_sq,
                    target_rows[offset : offset + col_size],
                    target_sq[offset : offset + col_size],
                )
            ) / entropic
            block_high = jnp.max(scores, axis=0)
            block_sum = jnp.sum(jnp.exp(scores - block_high[None, :]), axis=0)
            merged_high, merged_sum = combine_pairs(
                (carried[0][offset : offset + col_size], carried[1][offset : offset + col_size]),
                (block_high, block_sum),
            )
            new_high.append(merged_high)
            new_sum.append(merged_sum)
        return ((jnp.concatenate(new_high), jnp.concatenate(new_sum)), None)

    start_state = (
        jnp.full((total_cols,), -jnp.inf, jnp.float32),
        jnp.zeros((total_cols,), jnp.float32),
    )
    final_state, unused = lax.scan(
        target_one_block,
        start_state,
        (
            source_rows.reshape(row_count, row_size, source_rows.shape[1]),
            source_sq.reshape(row_count, row_size),
            source_pot.reshape(row_count, row_size),
        ),
    )
    return final_state


def on_device(source, target):
    source_rows = lax.all_gather(source, "col", axis=0, tiled=True)
    target_rows = lax.all_gather(target, "row", axis=0, tiled=True)
    source_sq = jnp.sum(jnp.square(source_rows.astype(jnp.float32)), axis=1)
    target_sq = jnp.sum(jnp.square(target_rows.astype(jnp.float32)), axis=1)
    log_targets = jnp.log(jnp.float32(target_rows.shape[0] * lax.axis_size("col")))
    log_sources = jnp.log(jnp.float32(source_rows.shape[0] * lax.axis_size("row")))
    target_pot = jnp.zeros((target_rows.shape[0],), jnp.float32)
    source_pot = jnp.zeros((source_rows.shape[0],), jnp.float32)
    for sweep in range(ITERS):
        highest, summed = source_partials(
            source_rows, source_sq, target_rows, target_sq, target_pot
        )
        overall = lax.pmax(highest, "col")
        summed = lax.psum(summed * jnp.exp(highest - overall), "col")
        highest = overall
        source_pot = entropic * (log_targets - highest - jnp.log(summed))
        highest, summed = target_partials(
            source_rows, source_sq, target_rows, target_sq, source_pot
        )
        overall = lax.pmax(highest, "row")
        summed = lax.psum(summed * jnp.exp(highest - overall), "row")
        target_pot = entropic * (log_sources - overall - jnp.log(summed))
    return (source_pot, target_pot)


def solution(mesh):
    placed = (P(("row", "col"), None), P(("col", "row"), None))
    return jax.shard_map(
        on_device, mesh=mesh, in_specs=placed, out_specs=(P("row"), P("col")), check_vma=False
    )
```

profile of v0, /device:TPU:0, one launch (start us, length us, event | category | flops | bytes accessed | tf_op | source)
XLA Modules:
  0.0 913.6 jit_solution(18065330960589869503)
XLA Ops:
  8.6 26.9 %all-gather.3.cloned.1.call-done = bf16[4096,128]{1,0:T(8,128)(2,1)} async-done(((bf16[512,128]{1,0:T(8,128)(2,1)}), bf16[4096,128]{1,0:T(8,128)(2,1)}) %all-gather.3.cloned.1.call-update) | async-done | bytes 1048592 | tf_op jit(solution)/shard_map/all_gather | solution.py:109
  35.6 1.9 multiply_reduce_fusion.1
  37.5 42.9 %all-gather.5.cloned.1.call-done = bf16[4096,128]{1,0:T(8,128)(2,1)} async-done(((bf16[256,128]{1,0:T(8,128)(2,1)}), bf16[4096,128]{1,0:T(8,128)(2,1)}) %all-gather.5.cloned.1.call-update) | async-done | bytes 1048592 | tf_op jit(solution)/shard_map/all_gather | solution.py:110
  80.5 1.8 multiply_reduce_fusion
  82.3 47.6 %while.72 = (s32[]{:T(128)}, f32[8,512]{1,0:T(8,128)S(1)}, f32[8,512]{1,0:T(8,128)S(1)}, f32[8,512]{1,0:T(8,128)S(1)}, f32[4096]{0:T(1024)S(1)}, /*index=5*/bf16...) while((s32[]{:T(128)}, f32[8,512]{1,0:T(8,128)S(1)}, ...), condition=%wide.region_11.12_spmd, body=%wide.region_2.11_spmd.sunk | while | flops 553655808 | bytes 22673564 | solution.py:51
  82.4 1.7 fusion.165
  88.3 1.7 fusion.165
  94.3 1.7 fusion.165
  100.2 1.7 fusion.165
  106.2 1.7 fusion.165
  112.1 1.7 fusion.165
  118.1 1.7 fusion.165
  124.1 1.7 fusion.165
  130.0 24.1 %pmax.42 = f32[4096]{0:T(1024)S(1)} all-reduce(f32[4096]{0:T(1024)S(1)} %bitcast.296), channel_id=1, replica_groups=mesh['row'=16,'col'=8] {'col'}, use_global_device_ids=true, to_apply=%region_12.13 | all-reduce | flops 4096 | bytes 32768 | tf_op jit(solution)/shard_map/pmax | solution.py:121
  154.1 23.6 %psum.42 = f32[4096]{0:T(1024)S(1)} all-reduce(f32[4096]{0:T(1024)S(1)} %exponential_multiply_fusion.5), channel_id=1, replica_groups=mesh['row'=16,'col'=8] {'col'}, use_global_device_ids=true, to_apply=%region_13.14 | all-reduce | flops 4096 | bytes 32768 | tf_op jit(solution)/shard_map/psum | solution.py:122
  177.7 39.0 %while.73 = (s32[]{:T(128)}, f32[4096]{0:T(1024)S(1)}, f32[4096]{0:T(1024)S(1)}, f32[8,512]{1,0:T(8,128)S(1)}, f32[8,512]{1,0:T(8,128)S(1)}, /*index=5*/f32[4096...) while((s32[]{:T(128)}, f32[4096]{0:T(1024)S(1)}, ...), condition=%wide.region_23.24_spmd, body=%wide.region_14.23_spmd.sunk | while | flops 553690112 | bytes 22839444 | solution.py:96
  177.8 1.6 fusion.171
  216.8 72.4 %pmax.43 = f32[4096]{0:T(1024)S(1)} all-reduce(f32[4096]{0:T(1024)S(1)} %get-tuple-element.257), channel_id=1, replica_groups=mesh['row'=16,'col'=8] {'row'}, use_global_device_ids=true, to_apply=%region_24.25 | all-reduce | flops 4096 | bytes 32768 | tf_op jit(solution)/shard_map/pmax | solution.py:128
  289.1 69.7 %psum.43 = f32[4096]{0:T(1024)S(1)} all-reduce(f32[4096]{0:T(1024)S(1)} %exponential_multiply_fusion.4), channel_id=1, replica_groups=mesh['row'=16,'col'=8] {'row'}, use_global_device_ids=true, to_apply=%region_25.26 | all-reduce | flops 4096 | bytes 32768 | tf_op jit(solution)/shard_map/psum | solution.py:129
  358.9 47.9 %while.74 = (s32[]{:T(128)}, f32[8,512]{1,0:T(8,128)S(1)}, f32[8,512]{1,0:T(8,128)S(1)}, f32[4096]{0:T(1024)S(1)}, f32[8,512]{1,0:T(8,128)S(1)}, /*index=5*/f32[...) while((s32[]{:T(128)}, f32[8,512]{1,0:T(8,128)S(1)}, ...), condition=%wide.region_35.36_spmd, body=%wide.region_26.35_spmd.sunk | while | flops 553655808 | bytes 22722724 | solution.py:51
  358.9 1.7 fusion.176
  364.9 1.7 fusion.176
  370.9 1.7 fusion.176
  376.9 1.7 fusion.176
  382.9 1.7 fusion.176
  388.9 1.7 fusion.176
  394.9 1.7 fusion.176
  400.8 1.7 fusion.176
  406.8 23.6 %pmax.44 = f32[4096]{0:T(1024)S(1)} all-reduce(f32[4096]{0:T(1024)S(1)} %bitcast.298), channel_id=1, replica_groups=mesh['row'=16,'col'=8] {'col'}, use_global_device_ids=true, to_apply=%region_36.37 | all-reduce | flops 4096 | bytes 32768 | tf_op jit(solution)/shard_map/pmax | solution.py:121
  430.4 23.6 %psum.44 = f32[4096]{0:T(1024)S(1)} all-reduce(f32[4096]{0:T(1024)S(1)} %exponential_multiply_fusion.3), channel_id=1, replica_groups=mesh['row'=16,'col'=8] {'col'}, use_global_device_ids=true, to_apply=%region_37.38 | all-reduce | flops 4096 | bytes 32768 | tf_op jit(solution)/shard_map/psum | solution.py:122
  454.0 39.0 %while.75 = (s32[]{:T(128)}, f32[4096]{0:T(1024)S(1)}, f32[4096]{0:T(1024)S(1)}, f32[8,512]{1,0:T(8,128)S(1)}, f32[8,512]{1,0:T(8,128)S(1)}, /*index=5*/f32[4096...) while((s32[]{:T(128)}, f32[4096]{0:T(1024)S(1)}, ...), condition=%wide.region_47.48_spmd, body=%wide.region_38.47_spmd.sunk | while | flops 553690112 | bytes 22839444 | solution.py:96
  493.0 69.5 %pmax.45 = f32[4096]{0:T(1024)S(1)} all-reduce(f32[4096]{0:T(1024)S(1)} %get-tuple-element.261), channel_id=1, replica_groups=mesh['row'=16,'col'=8] {'row'}, use_global_device_ids=true, to_apply=%region_48.49 | all-reduce | flops 4096 | bytes 32768 | tf_op jit(solution)/shard_map/pmax | solution.py:128
  562.5 69.7 %psum.45 = f32[4096]{0:T(1024)S(1)} all-reduce(f32[4096]{0:T(1024)S(1)} %exponential_multiply_fusion.2), channel_id=1, replica_groups=mesh['row'=16,'col'=8] {'row'}, use_global_device_ids=true, to_apply=%region_49.50 | all-reduce | flops 4096 | bytes 32768 | tf_op jit(solution)/shard_map/psum | solution.py:129
  632.3 47.8 %while.76 = (s32[]{:T(128)}, f32[8,512]{1,0:T(8,128)S(1)}, f32[8,512]{1,0:T(8,128)S(1)}, f32[4096]{0:T(1024)S(1)}, f32[8,512]{1,0:T(8,128)S(1)}, /*index=5*/f32[...) while((s32[]{:T(128)}, f32[8,512]{1,0:T(8,128)S(1)}, ...), condition=%wide.region_59.60_spmd, body=%wide.region_50.59_spmd.sunk | while | flops 553655808 | bytes 22722724 | solution.py:51
  632.4 1.7 fusion.187
  638.3 1.7 fusion.187
  644.3 1.7 fusion.187
  650.3 1.7 fusion.187
  656.3 1.7 fusion.187
  662.3 1.7 fusion.187
  668.2 1.7 fusion.187
  674.2 1.7 fusion.187
  680.2 23.6 %pmax.46 = f32[4096]{0:T(1024)S(1)} all-reduce(f32[4096]{0:T(1024)S(1)} %bitcast.300), channel_id=1, replica_groups=mesh['row'=16,'col'=8] {'col'}, use_global_device_ids=true, to_apply=%region_60.61 | all-reduce | flops 4096 | bytes 32768 | tf_op jit(solution)/shard_map/pmax | solution.py:121
  703.8 23.6 %psum.46 = f32[4096]{0:T(1024)S(1)} all-reduce(f32[4096]{0:T(1024)S(1)} %exponential_multiply_fusion.1), channel_id=1, replica_groups=mesh['row'=16,'col'=8] {'col'}, use_global_device_ids=true, to_apply=%region_61.62 | all-reduce | flops 4096 | bytes 32768 | tf_op jit(solution)/shard_map/psum | solution.py:122
  727.9 39.1 %while.77 = (s32[]{:T(128)}, f32[4096]{0:T(1024)S(1)}, f32[4096]{0:T(1024)S(1)}, f32[8,512]{1,0:T(8,128)S(1)}, f32[8,512]{1,0:T(8,128)S(1)}, /*index=5*/f32[4096...) while((s32[]{:T(128)}, f32[4096]{0:T(1024)S(1)}, ...), condition=%wide.region_71.72_spmd, body=%wide.region_62.71_spmd.sunk | while | flops 553690112 | bytes 22839444 | solution.py:96
  737.7 1.6 fusion.193
  767.0 69.6 %pmax.47 = f32[4096]{0:T(1024)S(1)} all-reduce(f32[4096]{0:T(1024)S(1)} %get-tuple-element.265), channel_id=1, replica_groups=mesh['row'=16,'col'=8] {'row'}, use_global_device_ids=true, to_apply=%region_72.73 | all-reduce | flops 4096 | bytes 32768 | tf_op jit(solution)/shard_map/pmax | solution.py:128
  836.6 69.5 %psum.47 = f32[4096]{0:T(1024)S(1)} all-reduce(f32[4096]{0:T(1024)S(1)} %exponential_multiply_fusion), channel_id=1, replica_groups=mesh['row'=16,'col'=8] {'row'}, use_global_device_ids=true, to_apply=%region_73.74 | all-reduce | flops 4096 | bytes 32768 | tf_op jit(solution)/shard_map/psum | solution.py:129
  (784 shorter events, 215.3 us)
Async XLA Ops:
  7.2 28.4 %all-gather.3.cloned.1.call-start = ((), (), s32[]{:S(2)}) async-start(), calls=%async_computation | async-start | bytes 1179648 | tf_op jit(solution)/shard_map/all_gather | solution.py:109
  7.9 72.6 %all-gather.5.cloned.1.call-start = ((), (), s32[]{:S(2)}) async-start(), calls=%async_computation.1 | async-start | bytes 1114112 | tf_op jit(solution)/shard_map/all_gather | solution.py:110
  35.6 46.7 %copy-start = (bf16[4096,128]{1,0:T(8,128)(2,1)S(1)}, bf16[4096,128]{1,0:T(8,128)(2,1)}, u32[]{:S(2)}) copy-start(bf16[4096,128]{1,0:T(8,128)(2,1)} %all-gather.3.cloned.1.call-done) | copy-start | bytes 3145732
  82.4 2.2 copy-start.1
  88.3 2.2 copy-start.1
  94.3 2.2 copy-start.1
  100.2 2.2 copy-start.1
  106.2 2.2 copy-start.1
  112.1 2.2 copy-start.1
  118.1 2.2 copy-start.1
  124.0 2.2 copy-start.1
  177.8 2.0 copy-start.2
  182.7 2.0 copy-start.2
  187.5 2.0 copy-start.2
  192.4 2.0 copy-start.2
  197.3 2.0 copy-start.2
  202.2 2.0 copy-start.2
  211.9 2.0 copy-start.2
  358.9 2.2 copy-start.3
  364.9 2.2 copy-start.3
  370.9 2.2 copy-start.3
  376.9 2.2 copy-start.3
  382.9 2.2 copy-start.3
  388.9 2.2 copy-start.3
  394.8 2.2 copy-start.3
  400.8 2.2 copy-start.3
  454.0 2.0 copy-start.4
  463.8 2.0 copy-start.4
  468.7 2.0 copy-start.4
  473.5 2.0 copy-start.4
  478.4 2.0 copy-start.4
  483.3 2.0 copy-start.4
  488.2 2.0 copy-start.4
  632.4 2.2 copy-start.5
  638.3 2.2 copy-start.5
  644.3 2.2 copy-start.5
  650.3 2.2 copy-start.5
  656.3 2.2 copy-start.5
  662.3 2.2 copy-start.5
  668.2 2.2 copy-start.5
  674.2 2.2 copy-start.5
  732.9 2.0 copy-start.6
  737.7 2.0 copy-start.6
  742.6 2.0 copy-start.6
  747.5 2.0 copy-start.6
  752.4 2.0 copy-start.6
  757.3 2.0 copy-start.6
  762.2 2.0 copy-start.6
  (4 other events, 6.6 us)
Sparse Core Ops, SparseCore 0:
  9.7 25.8 all-gather.2
  37.7 42.6 all-gather.4
where the time goes:
time: 915 us; the launch traced here: 914 us
  blocking collectives  562 us (61%)
  matrix products  169 us (18%)
  other arithmetic  88.1 us (10%)
  waiting for transfers between devices  71.2 us (8%)
  between operations  14.3 us (2%)
    pmax x3, blocking collectives, on_device(): overall = lax.pmax(highest, 'row')  211 us
    psum x3, blocking collectives, on_device(): summed = lax.psum(summed * jnp.exp(highest - overall), 'row')  209 us
    dot_general x192, matrix products, pair_cost(): lax.dot_general(source_block, target_block, (((1,), (1,)), ((), ())), pre...  169 us
    pmax x3, blocking collectives, on_device(): overall = lax.pmax(highest, 'col')  71.2 us
    psum x3, blocking collectives, on_device(): summed = lax.psum(summed * jnp.exp(highest - overall), 'col')  70.7 us
    reduce_sum x96, other arithmetic, source_one_block(): block_sum = jnp.sum(jnp.exp(scores - block_high[:, None]), axis=1)  49.5 us
    all_gather x1, waiting for transfers between devices, on_device(): target_rows = lax.all_gather(target, 'row', axis=0, tiled=True)  42.9 us
    reduce_sum x96, other arithmetic, target_one_block(): block_sum = jnp.sum(jnp.exp(scores - block_high[None, :]), axis=0)  32.4 us
  transfers between devices with their start and end apart: 2, of which 2 were waited for; matrix products, arithmetic and copies ran while one was open for 0% of the time, Pallas kernels for 0%

commit v1 on v0

v1 whole, which is shorter than its diff:
```python
import functools
import math

import jax
import jax.numpy as jnp
from jax import lax
from jax.experimental import pallas as pl
from jax.experimental.pallas import tpu as pltpu
from jax.sharding import PartitionSpec as P

ITERS = 3
EPS = 0.02
LOG2E = 1.0 / math.log(2.0)
SCALE = 2.0 * LOG2E / EPS
BACK = EPS / LOG2E
F32 = jnp.float32
BF16 = jnp.bfloat16
MESH = pl.DeviceIdType.MESH


def log2(x):
    return jnp.log(x) * LOG2E


def split3(x):
    high = x.astype(BF16).astype(F32)
    mid = (x - high).astype(BF16).astype(F32)
    return high, mid, x - high - mid


def pick3(x, index):
    high, mid, low = split3(x)
    zero = jnp.zeros_like(high)
    return jnp.where(
        index == 0, high, jnp.where(index == 1, mid, jnp.where(index == 2, low, zero))
    ).astype(BF16)


def nt_dot(x, y):
    return lax.dot_general(x, y, (((1,), (1,)), ((), ())), preferred_element_type=F32)


def kernel(
    row_n, col_n, s_ref, t_ref, f_ref, g_ref,
    s_all, t_all, s_ext, t_ext, kept, z0, z1, part, col_high, s_sq, t_sq, from_col, from_row,
    s_send, s_recv, t_send, t_recv, col_send, col_recv, row_send, row_recv,
):
    own_s, depth = s_ref.shape
    own_t = t_ref.shape[0]
    ns, nt = own_s * col_n, own_t * row_n
    total_s, total_t = float(ns * row_n), float(nt * col_n)
    my_row, my_col = lax.axis_index("row"), lax.axis_index("col")
    col_peers = [lax.rem(my_col + k, col_n) for k in range(1, col_n)]
    row_peers = [lax.rem(my_row + k, row_n) for k in range(1, row_n)]

    barrier = pltpu.get_barrier_semaphore()
    for peer in col_peers:
        pl.semaphore_signal(barrier, inc=1, device_id={"col": peer}, device_id_type=MESH)
    for peer in row_peers:
        pl.semaphore_signal(barrier, inc=1, device_id={"row": peer}, device_id_type=MESH)
    pl.semaphore_wait(barrier, col_n + row_n - 2)

    s_rows = pl.ds(pl.multiple_of(my_col * own_s, own_s), own_s)
    t_rows = pl.ds(pl.multiple_of(my_row * own_t, own_t), own_t)
    gathers = []
    for k, peer in enumerate(row_peers):
        gathers.append(
            pltpu.make_async_remote_copy(
                t_ref, t_all.at[t_rows, :], t_send.at[k], t_recv.at[k],
                device_id={"row": peer}, device_id_type=MESH,
            )
        )
    for k, peer in enumerate(col_peers):
        gathers.append(
            pltpu.make_async_remote_copy(
                s_ref, s_all.at[s_rows, :], s_send.at[k], s_recv.at[k],
                device_id={"col": peer}, device_id_type=MESH,
            )
        )
    for copy in gathers:
        copy.start()
    s_all[s_rows, :] = s_ref[...]
    t_all[t_rows, :] = t_ref[...]
    for copy in gathers:
        copy.wait()

    chunk = min(512, own_s, own_t)
    lane = lax.broadcasted_iota(jnp.int32, (chunk, depth), 1)
    ones = jnp.where(lane < 3, 1.0, 0.0).astype(BF16)

    def s_prepare(i, _):
        rows = pl.ds(pl.multiple_of(i * chunk, chunk), chunk)
        x = s_all[rows, :].astype(F32)
        s_sq[:, rows] = jnp.sum(jnp.transpose(x * x), axis=0, keepdims=True)
        s_ext[rows, :] = ones
        return 0

    def t_prepare(i, _):
        rows = pl.ds(pl.multiple_of(i * chunk, chunk), chunk)
        x = t_all[rows, :].astype(F32)
        t_sq[:, rows] = jnp.sum(jnp.transpose(x * x), axis=0, keepdims=True)
        bias = jnp.sum(x * x, axis=1, keepdims=True) * -0.5
        t_ext[rows, :] = pick3(jnp.broadcast_to(bias, (chunk, depth)), lane)
        return 0

    lax.fori_loop(0, ns // chunk, s_prepare, 0)
    lax.fori_loop(0, nt // chunk, t_prepare, 0)

    def logs_pass(x_all, x_ext, w_all, w_ext, out, keep):
        nx, nw = x_all.shape[0], w_all.shape[0]
        width = z0.shape[1]
        tiles = nw // width
        step = min(512, nx)
        fine = min(64, step)

        def lanes(tile):
            return pl.ds(pl.multiple_of(tile * width, width), width)

        def scores(tile, q, z, highest):
            rows = pl.ds(q * step, step)
            at = lanes(tile)
            x = jnp.concatenate([x_all[rows, :], x_ext[rows, :]], axis=1)
            w = jnp.concatenate([w_all[at, :], w_ext[at, :]], axis=1)
            inner = nt_dot(x, w)
            z[rows, :] = inner
            return jnp.maximum(highest, jnp.max(inner.reshape(step // 8, 8, width), axis=0))

        def sums(tile, q, z, highest, summed):
            for j in range(q * step, (q + 1) * step, fine):
                rows = pl.ds(j, fine)
                shifted = z[rows, :].reshape(fine // 8, 8, width) - highest[None]
                terms = jnp.exp2(shifted * SCALE)
                if keep:
                    kept[rows, lanes(tile)] = terms.reshape(fine, width).astype(BF16)
                summed = summed + jnp.sum(terms, axis=0)
            return summed

        def settle(highest):
            return jnp.broadcast_to(jnp.max(highest, axis=0, keepdims=True), (8, width))

        low = jnp.full((8, width), -3e38, F32)

        def both(tile, z_now, highest, z_next):
            following = jnp.minimum(tile + 1, tiles - 1)
            new_high = low
            summed = jnp.zeros((8, width), F32)
            for q in range(nx // step):
                new_high = scores(following, q, z_next, new_high)
                summed = sums(tile, q, z_now, highest, summed)
            top = highest[0:1, :] * SCALE
            out[:, lanes(tile)] = top + log2(jnp.sum(summed, axis=0, keepdims=True))
            if keep:
                col_high[:, lanes(tile)] = top
            return settle(new_high)

        def pair(i, highest):
            highest = both(2 * i, z0, highest, z1)
            return both(2 * i + 1, z1, highest, z0)

        first = low
        for q in range(nx // step):
            first = scores(0, q, z0, first)
        lax.fori_loop(0, tiles // 2, pair, settle(first))

    def exchange(turn, sent, received, send, recv, axis, peers):
        copies = [
            pltpu.make_async_remote_copy(
                sent, received.at[turn, k], send.at[turn, k], recv.at[turn, k],
                device_id={axis: peer}, device_id_type=MESH,
            )
            for k, peer in enumerate(peers)
        ]
        for copy in copies:
            copy.start()
        for copy in copies:
            copy.wait()
        return [sent[...]] + [received[turn, k] for k in range(len(peers))]

    def over_col(turn):
        return exchange(turn, part.at[2 * turn], from_col, col_send, col_recv, "col", col_peers)

    def over_row(turn):
        return exchange(turn, part.at[2 * turn + 1], from_row, row_send, row_recv, "row", row_peers)

    def combined_logs(logs):
        highest = functools.reduce(jnp.maximum, logs)
        return highest + log2(sum(jnp.exp2(x - highest) for x in logs))

    logs_pass(t_all, t_ext, s_all, s_ext, part.at[0], False)
    f_first = math.log2(total_t) - combined_logs(over_col(0))
    f_ref[...] = f_first

    def s_bias(i, _):
        rows = pl.ds(pl.multiple_of(i * chunk, chunk), chunk)
        bias = jnp.transpose(jnp.broadcast_to(f_ref[:, rows] * (1.0 / SCALE), (depth, chunk)))
        s_ext[rows, :] = pick3(bias, lane)
        return 0

    def t_ones(i, _):
        t_ext[pl.ds(pl.multiple_of(i * chunk, chunk), chunk), :] = ones
        return 0

    lax.fori_loop(0, ns // chunk, s_bias, 0)
    lax.fori_loop(0, nt // chunk, t_ones, 0)
    logs_pass(s_all, s_ext, t_all, t_ext, part.at[1], True)
    g_first = math.log2(total_s) - combined_logs(over_row(0))
    g_ref[...] = g_first
    col_high[...] = jnp.exp2(g_first + col_high[...])

    block = min(512, ns, nt)

    def parts_of(x):
        return pick3(jnp.broadcast_to(x, (16, x.shape[1])), lax.broadcasted_iota(jnp.int32, (16, x.shape[1]), 0))

    def row_sums(x, out):
        lhs = parts_of(x)

        def one(i, _):
            rows = pl.ds(pl.multiple_of(i * block, block), block)
            out[:, rows] = jnp.sum(nt_dot(lhs, kept[rows, :]), axis=0, keepdims=True)
            return 0

        lax.fori_loop(0, ns // block, one, 0)

    def col_sums(x, out):
        lhs = parts_of(x)

        def one(i, _):
            at = pl.ds(pl.multiple_of(i * block, block), block)
            found = jnp.dot(lhs, kept[:, at], preferred_element_type=F32)
            out[:, at] = jnp.sum(found, axis=0, keepdims=True) * col_high[:, at]
            return 0

        lax.fori_loop(0, nt // block, one, 0)

    weight = col_high[...]
    for turn in range(1, ITERS):
        row_sums(weight, part.at[2 * turn])
        u = total_t / sum(over_col(turn))
        col_sums(u, part.at[2 * turn + 1])
        v = total_s / sum(over_row(turn))
        weight = col_high[...] * v
    f_ref[...] = BACK * (f_ref[...] + log2(u)) + s_sq[...]
    g_ref[...] = BACK * (g_ref[...] + log2(v)) + t_sq[...]


def on_device(row_n, col_n, source, target):
    own_s, depth = source.shape
    own_t = target.shape[0]
    ns, nt = own_s * col_n, own_t * row_n
    width = min(256, ns // 2, nt // 2)
    vmem = pl.BlockSpec(memory_space=pltpu.VMEM)
    dma = pltpu.SemaphoreType.DMA
    f, g = pl.pallas_call(
        functools.partial(kernel, row_n, col_n),
        out_shape=(jax.ShapeDtypeStruct((1, ns), F32), jax.ShapeDtypeStruct((1, nt), F32)),
        in_specs=[vmem, vmem],
        out_specs=(vmem, vmem),
        scratch_shapes=[
            pltpu.VMEM((ns, depth), BF16),
            pltpu.VMEM((nt, depth), BF16),
            pltpu.VMEM((ns, depth), BF16),
            pltpu.VMEM((nt, depth), BF16),
            pltpu.VMEM((ns, nt), BF16),
            pltpu.VMEM((max(ns, nt), width), F32),
            pltpu.VMEM((max(ns, nt), width), F32),
            pltpu.VMEM((2 * ITERS, 1, max(ns, nt)), F32),
            pltpu.VMEM((1, nt), F32),
            pltpu.VMEM((1, ns), F32),
            pltpu.VMEM((1, nt), F32),
            pltpu.VMEM((ITERS, col_n - 1, 1, ns), F32),
            pltpu.VMEM((ITERS, row_n - 1, 1, nt), F32),
            dma((col_n - 1,)),
            dma((col_n - 1,)),
            dma((row_n - 1,)),
            dma((row_n - 1,)),
            dma((ITERS, col_n - 1)),
            dma((ITERS, col_n - 1)),
            dma((ITERS, row_n - 1)),
            dma((ITERS, row_n - 1)),
        ],
        compiler_params=pltpu.CompilerParams(
            collective_id=0, has_side_effects=True, vmem_limit_bytes=60 << 20
        ),
        cost_estimate=pl.CostEstimate(
            flops=12 * ns * nt * depth, bytes_accessed=2 * (ns + nt) * depth, transcendentals=2 * ns * nt
        ),
    )(source, target)
    return f.reshape(ns), g.reshape(nt)


def solution(mesh):
    placed = (P(("row", "col"), None), P(("col", "row"), None))
    return jax.shard_map(
        functools.partial(on_device, mesh.shape["row"], mesh.shape["col"]),
        mesh=mesh,
        in_specs=placed,
        out_specs=(P("row"), P("col")),
        check_vma=False,
    )
```

time: 915 us -> 136 us (0.15)
  blocking collectives: 562 us -> 0 us
  matrix products: 169 us -> 0 us
  Pallas kernels: 0 us -> 132 us
  other arithmetic: 88.1 us -> 0 us
  waiting for transfers between devices: 71.2 us -> 0 us
  between operations: 14.3 us -> 0.65 us
    pmax x6 -> x0, blocking collectives: 283 us -> none  [the longest x3 211 us: on_device(): overall = lax.pmax(highest, 'row')]
    psum x6 -> x0, blocking collectives: 280 us -> none  [the longest x3 209 us: on_device(): summed = lax.psum(summed * jnp.exp(highest - overall), 'row')]
    dot_general x192 -> x0, matrix products: 169 us -> none  [pair_cost(): lax.dot_general(source_block, target_block, (((1,), (1,)), ((), ())), pre...]
    pallas_call x0 -> x1, Pallas kernels: none -> 132 us  [on_device(): pl.pallas_call(functools.partial(kernel, row_n, col_n), out_shape=(jax.Sh...]
    reduce_sum x194 -> x0, other arithmetic: 85.6 us -> none  [the longest x96 49.5 us: source_one_block(): block_sum = jnp.sum(jnp.exp(scores - block_high[:, None]), axis=1)]
    all_gather x2 -> x0, waiting for transfers between devices: 69.9 us -> none  [the longest x1 42.9 us: on_device(): target_rows = lax.all_gather(target, 'row', axis=0, tiled=True)]
  transfers between devices with their start and end apart: 2 -> 0, of which waited for: 2 -> 0; matrix products, arithmetic and copies ran while one was open for 0% -> 0% of each run, Pallas kernels for 0% -> 0%
where the time goes in v1:
time: 136 us; the launch traced here: 135 us
  Pallas kernels  132 us (97%)
  local copies, waits for them, and re-layouts  1.94 us (1%)
    pallas_call x1, Pallas kernels, on_device(): pl.pallas_call(functools.partial(kernel, row_n, col_n), out_shape=(jax.Sh...  132 us

profile of v1, /device:TPU:0, one launch (start us, length us, event | category | flops | bytes accessed | tf_op | source)
XLA Modules:
  0.0 135.0 jit_solution(4777708822815372554)
XLA Ops:
  0.6 132.4 %shard_map.41 = (f32[1,4096]{1,0:T(1,128)}, f32[1,4096]{1,0:T(1,128)}) custom-call(bf16[512,128]{1,0:T(8,128)(2,1)} %s_ref.1, bf16[256,128]{1,0:T(8,128)(2,1)} %t_ref.1), custom_call_target="tpu_custom_call" | custom-call | flops 25769803776 | bytes 2097152 | tf_op jit(solution)/shard_map/pallas_call | solution.py:254
  133.1 0.0 copy-start
  133.1 1.3 copy.6
  134.4 0.0 copy-done
  134.4 0.6 copy.7
Async XLA Ops:
  133.1 1.3 copy-start

commit v2 on v0

--- a/solution.py
+++ b/solution.py
@@ -1,12 +1,23 @@
+import functools
+import math
+
 import jax
 import jax.numpy as jnp
 from jax import lax
+from jax.experimental import pallas as pl
+from jax.experimental.pallas import tpu as pltpu
 from jax.sharding import PartitionSpec as P
 
 ITERS = 3
-
-
-entropic = 0.02
+EPS = 0.02
+LOG2E = 1.0 / math.log(2.0)
+SCALE = 2.0 * LOG2E / EPS
+BACK = EPS / LOG2E
+FLOOR = 90.0
+CEIL = 100.0
+F32 = jnp.float32
+BF16 = jnp.bfloat16
+MESH = pl.DeviceIdType.MESH
 
 
 def pair_cost(source_block, source_sq_block, target_block, target_sq_block):
@@ -42,7 +53,7 @@
                     target_rows[offset : offset + col_size],
                     target_sq[offset : offset + col_size],
                 )
-            ) / entropic
+            ) / EPS
             block_high = jnp.max(scores, axis=1)
             block_sum = jnp.sum(jnp.exp(scores - block_high[:, None]), axis=1)
             highest, summed = combine_pairs((highest, summed), (block_high, block_sum))
@@ -78,7 +89,7 @@
                     target_rows[offset : offset + col_size],
                     target_sq[offset : offset + col_size],
                 )
-            ) / entropic
+            ) / EPS
             block_high = jnp.max(scores, axis=0)
             block_sum = jnp.sum(jnp.exp(scores - block_high[None, :]), axis=0)
             merged_high, merged_sum = combine_pairs(
@@ -105,7 +116,7 @@
     return final_state
 
 
-def on_device(source, target):
+def careful(source, target):
     source_rows = lax.all_gather(source, "col", axis=0, tiled=True)
     target_rows = lax.all_gather(target, "row", axis=0, tiled=True)
     source_sq = jnp.sum(jnp.square(source_rows.astype(jnp.float32)), axis=1)
@@ -121,18 +132,368 @@
         overall = lax.pmax(highest, "col")
         summed = lax.psum(summed * jnp.exp(highest - overall), "col")
         highest = overall
-        source_pot = entropic * (log_targets - highest - jnp.log(summed))
+        source_pot = EPS * (log_targets - highest - jnp.log(summed))
         highest, summed = target_partials(
             source_rows, source_sq, target_rows, target_sq, source_pot
         )
         overall = lax.pmax(highest, "row")
         summed = lax.psum(summed * jnp.exp(highest - overall), "row")
-        target_pot = entropic * (log_sources - overall - jnp.log(summed))
+        target_pot = EPS * (log_sources - overall - jnp.log(summed))
     return (source_pot, target_pot)
+
+
+def log2(x):
+    return jnp.log(x) * LOG2E
+
+
+def split3(x):
+    high = x.astype(BF16).astype(F32)
+    mid = (x - high).astype(BF16).astype(F32)
+    return high, mid, x - high - mid
+
+
+def pick3(x, index, base, other):
+    high, mid, low = split3(x)
+    found = jnp.where(index == base + 1, mid, jnp.where(index == base + 2, low, other))
+    return jnp.where(index == base, high, found).astype(BF16)
+
+
+def nt_dot(x, y):
+    return lax.dot_general(x, y, (((1,), (1,)), ((), ())), preferred_element_type=F32)
+
+
+def kernel(
+    row_n, col_n, s_ref, t_ref, f_ref, g_ref,
+    s_all, t_all, s_ext, t_ext, kept, sums, highs, part, weight, s_sq, t_sq, shift_s, shift_t, from_col, from_row,
+    s_send, s_recv, t_send, t_recv, pair_send, pair_recv, col_send, col_recv, row_send, row_recv,
+):
+    own_s, depth = s_ref.shape
+    own_t = t_ref.shape[0]
+    ns, nt = own_s * col_n, own_t * row_n
+    total_s, total_t = float(ns * row_n), float(nt * col_n)
+    my_row, my_col = lax.axis_index("row"), lax.axis_index("col")
+    col_peers = [lax.rem(my_col + k, col_n) for k in range(1, col_n)]
+    row_peers = [lax.rem(my_row + k, row_n) for k in range(1, row_n)]
+    my_core = lax.rem(my_col, 2)
+    twin = my_col + 1 - 2 * my_core
+    chips = col_n // 2
+
+    barrier = pltpu.get_barrier_semaphore()
+    for peer in col_peers:
+        pl.semaphore_signal(barrier, inc=1, device_id={"col": peer}, device_id_type=MESH)
+    for peer in row_peers:
+        pl.semaphore_signal(barrier, inc=1, device_id={"row": peer}, device_id_type=MESH)
+
+    def s_block(index):
+        return pl.ds(pl.multiple_of(index * own_s, own_s), own_s)
+
+    def t_block(index):
+        return pl.ds(pl.multiple_of(index * own_t, own_t), own_t)
+
+    def s_from(k):
+        return lax.rem(my_col - 2 * k + col_n, col_n)
+
+    def twin_from(k):
+        return lax.rem(twin - 2 * k + col_n, col_n)
+
+    def t_from(k):
+        return lax.rem(my_row - k + row_n, row_n)
+
+    def t_copy(k):
+        return pltpu.make_async_remote_copy(
+            t_ref, t_all.at[t_block(my_row), :], t_send.at[k], t_recv.at[k],
+            device_id={"row": lax.rem(my_row + k, row_n)}, device_id_type=MESH,
+        )
+
+    def s_copy(k):
+        return pltpu.make_async_remote_copy(
+            s_ref, s_all.at[s_block(my_col), :], s_send.at[k], s_recv.at[k],
+            device_id={"col": lax.rem(my_col + 2 * k, col_n)}, device_id_type=MESH,
+        )
+
+    def twin_copy(k):
+        at = s_all.at[s_block(s_from(k)), :]
+        return pltpu.make_async_remote_copy(
+            at, at, pair_send.at[k], pair_recv.at[k], device_id={"col": twin}, device_id_type=MESH
+        )
+
+    chunk = 128
+    lane = lax.broadcasted_iota(jnp.int32, (chunk, depth), 1)
+    first_ones = jnp.where(lane < 3, 1.0, 0.0)
+    later_ones = jnp.where((lane >= 3) & (lane < 6), 1.0, 0.0)
+
+    def spread(column):
+        return jnp.broadcast_to(column, (chunk, depth))
+
+    def t_prepare(block):
+        def one(i, _):
+            rows = pl.ds(pl.multiple_of(block * own_t + i * chunk, chunk), chunk)
+            x = t_all[rows, :].astype(F32)
+            square = x * x
+            t_sq[:, rows] = jnp.sum(jnp.transpose(square), axis=0, keepdims=True)
+            bias = spread(jnp.sum(square, axis=1, keepdims=True) * -0.5)
+            t_ext[rows, :] = pick3(bias, lane, 0, later_ones)
+            highs[rows, :] = jnp.full((chunk, depth), -3e38, F32)
+            return 0
+
+        lax.fori_loop(0, own_t // chunk, one, 0)
+
+    def s_prepare(block):
+        mine = t_block(my_row)
+        sample = jnp.concatenate([t_ref[...], t_ext[mine, :]], axis=1)
+
+        def one(i, _):
+            rows = pl.ds(pl.multiple_of(block * own_s + i * chunk, chunk), chunk)
+            x = s_all[rows, :]
+            square = x.astype(F32) * x.astype(F32)
+            s_sq[:, rows] = jnp.sum(jnp.transpose(square), axis=0, keepdims=True)
+            seen = nt_dot(jnp.concatenate([x, first_ones.astype(BF16)], axis=1), sample)
+            shift = spread(-FLOOR / SCALE - jnp.max(seen, axis=1, keepdims=True))
+            shift_s[:, rows] = jnp.transpose(shift)[0:1, :]
+            s_ext[rows, :] = pick3(shift, lane, 3, first_ones)
+            return 0
+
+        lax.fori_loop(0, own_s // chunk, one, 0)
+
+    s_all[s_block(my_col), :] = s_ref[...]
+    t_all[t_block(my_row), :] = t_ref[...]
+    sums[...] = jnp.zeros_like(sums)
+    t_prepare(my_row)
+    s_prepare(my_col)
+
+    pl.semaphore_wait(barrier, col_n + row_n - 2)
+    for k in range(1, chips):
+        s_copy(k).start()
+    for k in range(1, row_n):
+        t_copy(k).start()
+    twin_copy(0).start()
+
+    per = 2
+
+    def terms_with(t_index, s_index):
+        x = jnp.concatenate(
+            [jnp.concatenate([t_all[t_block(i), :], t_ext[t_block(i), :]], axis=1) for i in t_index], axis=0
+        )
+        high = None
+        for i in s_index:
+            at = s_block(i)
+            z = nt_dot(x, jnp.concatenate([s_all[at, :], s_ext[at, :]], axis=1))
+            for c in range(0, own_s, depth):
+                piece = z[:, c : c + depth]
+                high = piece if high is None else jnp.maximum(high, piece)
+            terms = jnp.exp2(z * SCALE).reshape(z.shape[0] // 8, 8, own_s)
+            sums[:, at] = sums[:, at] + jnp.sum(terms, axis=0)
+        for n, i in enumerate(t_index):
+            at = t_block(i)
+            highs[at, :] = jnp.maximum(highs[at, :], high[n * own_t : (n + 1) * own_t, :])
+
+    for k in range(1, chips):
+        s_copy(k).wait_recv()
+        twin_copy(k).start()
+        s_prepare(s_from(k))
+
+    def near(p, _):
+        @pl.when(p > 0)
+        def _():
+            t_copy(per * p).wait_recv()
+            t_prepare(t_from(per * p))
+
+        for j in range(1, per):
+            t_copy(per * p + j).wait_recv()
+            t_prepare(t_from(per * p + j))
+        terms_with([t_from(per * p + j) for j in range(per)], [s_from(k) for k in range(chips)])
+        return 0
+
+    lax.fori_loop(0, row_n // per, near, 0)
+
+    for k in range(chips):
+        twin_copy(k).wait_recv()
+        s_prepare(twin_from(k))
+
+    def far(p, _):
+        terms_with([t_from(per * p + j) for j in range(per)], [twin_from(k) for k in range(chips)])
+        return 0
+
+    lax.fori_loop(0, row_n // per, far, 0)
+
+    for k in range(1, chips):
+        s_copy(k).wait_send()
+    for k in range(chips):
+        twin_copy(k).wait_send()
+    for k in range(1, row_n):
+        t_copy(k).wait_send()
+
+    def exchange(turn, sent, received, send, recv, axis, peers, meanwhile=None):
+        copies = [
+            pltpu.make_async_remote_copy(
+                sent, received.at[turn, k], send.at[turn, k], recv.at[turn, k],
+                device_id={axis: peer}, device_id_type=MESH,
+            )
+            for k, peer in enumerate(peers)
+        ]
+        for copy in copies:
+            copy.start()
+        if meanwhile is not None:
+            meanwhile()
+        for copy in copies:
+            copy.wait()
+        return [sent[...]] + [received[turn, k] for k in range(len(peers))]
+
+    def over_col(turn, meanwhile=None):
+        return exchange(turn, part.at[2 * turn], from_col, col_send, col_recv, "col", col_peers, meanwhile)
+
+    def over_row(turn):
+        return exchange(turn, part.at[2 * turn + 1], from_row, row_send, row_recv, "row", row_peers)
+
+    def combined_logs(logs):
+        highest = functools.reduce(jnp.maximum, logs)
+        return highest + log2(sum(jnp.exp2(x - highest) for x in logs))
+
+    def t_shift():
+        room = (FLOOR + math.log2(total_t) - CEIL) / SCALE
+
+        def one(i, _):
+            rows = pl.ds(pl.multiple_of(i * chunk, chunk), chunk)
+            bias = jnp.sum(jnp.where(lane < 3, t_ext[rows, :].astype(F32), 0.0), axis=1, keepdims=True)
+            shift = spread(bias - jnp.max(highs[rows, :], axis=1, keepdims=True) - room)
+            shift_t[:, rows] = jnp.transpose(shift)[0:1, :]
+            t_ext[rows, :] = pick3(shift, lane, 3, first_ones)
+            return 0
+
+        lax.fori_loop(0, nt // chunk, one, 0)
+
+    found = jnp.sum(sums[...], axis=0, keepdims=True)
+    logs = log2(found) - shift_s[...] * SCALE
+    part[0] = jnp.where(found < 2.0**120, logs, jnp.nan)
+    f_first = math.log2(total_t) - combined_logs(over_col(0, t_shift))
+    f_ref[...] = f_first
+
+    def s_bias(i, _):
+        rows = pl.ds(pl.multiple_of(i * chunk, chunk), chunk)
+        bias = jnp.transpose(jnp.broadcast_to(f_ref[:, rows] * (1.0 / SCALE), (depth, chunk)))
+        s_ext[rows, :] = pick3(bias, lane, 0, later_ones)
+        return 0
+
+    lax.fori_loop(0, ns // chunk, s_bias, 0)
+
+    width = min(512, nt)
+    step = min(2048, ns)
+
+    def second(i, _):
+        at = pl.ds(pl.multiple_of(i * width, width), width)
+        w = jnp.concatenate([t_all[at, :], t_ext[at, :]], axis=1)
+        summed = jnp.zeros((8, width), F32)
+        for q in range(ns // step):
+            rows = pl.ds(q * step, step)
+            terms = jnp.exp2(nt_dot(jnp.concatenate([s_all[rows, :], s_ext[rows, :]], axis=1), w) * SCALE)
+            kept[rows, at] = terms.astype(BF16)
+            summed = summed + jnp.sum(terms.reshape(step // 8, 8, width), axis=0)
+        part[1, :, at] = log2(jnp.sum(summed, axis=0, keepdims=True)) - shift_t[:, at] * SCALE
+        return 0
+
+    lax.fori_loop(0, nt // width, second, 0)
+    logs = combined_logs(over_row(0))
+    held = logs + shift_t[...] * SCALE
+    g_first = jnp.where(held > -30.0, math.log2(total_s) - logs, jnp.nan)
+    g_ref[...] = g_first
+    weight[0] = jnp.exp2(g_first - shift_t[...] * SCALE)
+    weight[1] = weight[0]
+
+    def row_sums(out):
+        fine = chunk // 2
+
+        def one(i, _):
+            pieces = []
+            for h in range(0, chunk, fine):
+                rows = pl.ds(pl.multiple_of(i * chunk, chunk) + h, fine)
+                summed = jnp.zeros((fine, 128), F32)
+                for c in range(0, nt, 128):
+                    summed = summed + kept[rows, c : c + 128].astype(F32) * weight[1, :, c : c + 128]
+                pieces.append(summed)
+            turned = jnp.transpose(jnp.concatenate(pieces, axis=0))
+            out[:, pl.ds(pl.multiple_of(i * chunk, chunk), chunk)] = jnp.sum(turned, axis=0, keepdims=True)
+            return 0
+
+        lax.fori_loop(0, ns // chunk, one, 0)
+
+    def col_sums(x, out):
+        wide = min(2048, nt)
+        index = lax.broadcasted_iota(jnp.int32, (16, ns), 0)
+        lhs = pick3(jnp.broadcast_to(x, (16, ns)), index, 0, 0.0)
+
+        def one(i, _):
+            at = pl.ds(pl.multiple_of(i * wide, wide), wide)
+            got = jnp.dot(lhs, kept[:, at], preferred_element_type=F32)
+            out[:, at] = jnp.sum(got, axis=0, keepdims=True) * weight[0, :, at]
+            return 0
+
+        lax.fori_loop(0, nt // wide, one, 0)
+
+    for turn in range(1, ITERS):
+        row_sums(part.at[2 * turn])
+        u = total_t / sum(over_col(turn))
+        col_sums(u, part.at[2 * turn + 1])
+        v = total_s / sum(over_row(turn))
+        weight[1] = weight[0] * v
+    f_ref[...] = BACK * (f_ref[...] + log2(u)) + s_sq[...]
+    g_ref[...] = BACK * (g_ref[...] + log2(v)) + t_sq[...]
+
+
+def on_device(row_n, col_n, source, target):
+    own_s, depth = source.shape
+    own_t = target.shape[0]
+    ns, nt = own_s * col_n, own_t * row_n
+    vmem = pl.BlockSpec(memory_space=pltpu.VMEM)
+    dma = pltpu.SemaphoreType.DMA
+    f, g = pl.pallas_call(
+        functools.partial(kernel, row_n, col_n),
+        out_shape=(jax.ShapeDtypeStruct((1, ns), F32), jax.ShapeDtypeStruct((1, nt), F32)),
+        in_specs=[vmem, vmem],
+        out_specs=(vmem, vmem),
+        scratch_shapes=[
+            pltpu.VMEM((ns, depth), BF16),
+            pltpu.VMEM((nt, depth), BF16),
+            pltpu.VMEM((ns, depth), BF16),
+            pltpu.VMEM((nt, depth), BF16),
+            pltpu.VMEM((ns, nt), BF16),
+            pltpu.VMEM((8, ns), F32),
+            pltpu.VMEM((nt, depth), F32),
+            pltpu.VMEM((2 * ITERS, 1, max(ns, nt)), F32),
+            pltpu.VMEM((2, 1, nt), F32),
+            pltpu.VMEM((1, ns), F32),
+            pltpu.VMEM((1, nt), F32),
+            pltpu.VMEM((1, ns), F32),
+            pltpu.VMEM((1, nt), F32),
+            pltpu.VMEM((ITERS, col_n - 1, 1, ns), F32),
+            pltpu.VMEM((ITERS, row_n - 1, 1, nt), F32),
+            dma((col_n // 2,)),
+            dma((col_n // 2,)),
+            dma((row_n,)),
+            dma((row_n,)),
+            dma((col_n // 2,)),
+            dma((col_n // 2,)),
+            dma((ITERS, col_n - 1)),
+            dma((ITERS, col_n - 1)),
+            dma((ITERS, row_n - 1)),
+            dma((ITERS, row_n - 1)),
+        ],
+        compiler_params=pltpu.CompilerParams(
+            collective_id=0, has_side_effects=True, vmem_limit_bytes=60 << 20
+        ),
+        cost_estimate=pl.CostEstimate(
+            flops=12 * ns * nt * depth, bytes_accessed=2 * (ns + nt) * depth, transcendentals=2 * ns * nt
+        ),
+    )(source, target)
+    fast = f.reshape(ns), g.reshape(nt)
+    return lax.cond(jnp.isnan(fast[0][0]), lambda: careful(source, target), lambda: fast)
 
 
 def solution(mesh):
     placed = (P(("row", "col"), None), P(("col", "row"), None))
     return jax.shard_map(
-        on_device, mesh=mesh, in_specs=placed, out_specs=(P("row"), P("col")), check_vma=False
+        functools.partial(on_device, mesh.shape["row"], mesh.shape["col"]),
+        mesh=mesh,
+        in_specs=placed,
+        out_specs=(P("row"), P("col")),
+        check_vma=False,
     )

time: 915 us -> 1040 us (1.14)
  Pallas kernels: 0 us -> 115 us
    pallas_call x0 -> x1, Pallas kernels: none -> 115 us  [on_device(): pl.pallas_call(functools.partial(kernel, row_n, col_n), out_shape=(jax.Sh...]
where the time goes in v2:
time: 1040 us; the launch traced here: 1030 us
  blocking collectives  562 us (54%)
  matrix products  169 us (16%)
  Pallas kernels  115 us (11%)
  other arithmetic  88.1 us (8%)
  waiting for transfers between devices  66.4 us (6%)
  between operations  15.6 us (2%)
    pmax x3, blocking collectives, careful(): overall = lax.pmax(highest, 'row')  211 us
    psum x3, blocking collectives, careful(): summed = lax.psum(summed * jnp.exp(highest - overall), 'row')  209 us
    dot_general x192, matrix products, pair_cost(): lax.dot_general(source_block, target_block, (((1,), (1,)), ((), ())), pre...  169 us
    pallas_call x1, Pallas kernels, on_device(): pl.pallas_call(functools.partial(kernel, row_n, col_n), out_shape=(jax.Sh...  115 us
    pmax x3, blocking collectives, careful(): overall = lax.pmax(highest, 'col')  71.2 us
    psum x3, blocking collectives, careful(): summed = lax.psum(summed * jnp.exp(highest - overall), 'col')  70.7 us
    reduce_sum x96, other arithmetic, source_one_block(): block_sum = jnp.sum(jnp.exp(scores - block_high[:, None]), axis=1)  49.5 us
    all_gather x1, waiting for transfers between devices, careful(): target_rows = lax.all_gather(target, 'row', axis=0, tiled=True)  42.9 us
  transfers between devices with their start and end apart: 2, of which 2 were waited for; matrix products, arithmetic and copies ran while one was open for 0% of the time, Pallas kernels for 0%

profile of v2, /device:TPU:0, one launch (start us, length us, event | category | flops | bytes accessed | tf_op | source)
XLA Modules:
  0.0 1029.4 jit_solution(14910927648446599076)
XLA Ops:
  7.2 115.2 %shard_map.45 = (f32[1,4096]{1,0:T(1,128)S(1)}, f32[1,4096]{1,0:T(1,128)}) custom-call(bf16[512,128]{1,0:T(8,128)(2,1)} %s_ref.1, bf16[256,128]{1,0:T(8,128)(2,1)} %t_ref.1), custom_call_target="tpu_custom_call" | custom-call | flops 25769803776 | bytes 2097152 | tf_op jit(solution)/shard_map/pallas_call | solution.py:448
  124.2 895.4 %conditional.1 = (f32[4096]{0:T(1024)}, f32[4096]{0:T(1024)}) conditional(s32[]{:T(128)} %bitcast.42, (f32[1,4096]{1,0:T(1,128)}, f32[1,4096]{1,0:T(1,128)}) %tuple.306, (bf16[512,128]{1,0:T(8,128)(2,1)}, bf16[256,128]{1,0:T(8,128)(2,1)}) %tuple.39), branch_computations={%region_0.0_spmd, %region_1.76_spmd} | conditional | flops 3325347328 | bytes 151514704 | solution.py:488
  125.7 22.6 %all-gather.3.cloned.1.call-done = bf16[4096,128]{1,0:T(8,128)(2,1)} async-done(((bf16[512,128]{1,0:T(8,128)(2,1)}), bf16[4096,128]{1,0:T(8,128)(2,1)}) %all-gather.3.cloned.1.call-update) | async-done | bytes 1048592 | tf_op jit(solution)/shard_map/cond/branch_1_fun/all_gather | solution.py:120
  148.3 1.9 multiply_reduce_fusion.1
  150.2 42.9 %all-gather.5.cloned.1.call-done = bf16[4096,128]{1,0:T(8,128)(2,1)} async-done(((bf16[256,128]{1,0:T(8,128)(2,1)}), bf16[4096,128]{1,0:T(8,128)(2,1)}) %all-gather.5.cloned.1.call-update) | async-done | bytes 1048592 | tf_op jit(solution)/shard_map/cond/branch_1_fun/all_gather | solution.py:121
  193.1 1.8 multiply_reduce_fusion
  195.0 47.6 %while.66 = (s32[]{:T(128)}, f32[8,512]{1,0:T(8,128)S(1)}, f32[8,512]{1,0:T(8,128)S(1)}, f32[8,512]{1,0:T(8,128)S(1)}, f32[4096]{0:T(1024)S(1)}, /*index=5*/bf16...) while((s32[]{:T(128)}, f32[8,512]{1,0:T(8,128)S(1)}, ...), condition=%wide.region_13.13_spmd, body=%wide.region_4.12_spmd.sunk | while | flops 553655808 | bytes 22673564 | solution.py:62
  195.1 1.7 fusion.165
  201.0 1.7 fusion.165
  207.0 1.7 fusion.165
  212.9 1.7 fusion.165
  218.9 1.7 fusion.165
  224.8 1.7 fusion.165
  230.8 1.7 fusion.165
  236.7 1.7 fusion.165
  242.7 24.1 %pmax.36 = f32[4096]{0:T(1024)S(1)} all-reduce(f32[4096]{0:T(1024)S(1)} %bitcast.299), channel_id=1, replica_groups=mesh['row'=16,'col'=8] {'col'}, use_global_device_ids=true, to_apply=%region_14.14 | all-reduce | flops 4096 | bytes 32768 | tf_op jit(solution)/shard_map/cond/branch_1_fun/pmax | solution.py:132
  266.8 23.6 %psum.36 = f32[4096]{0:T(1024)S(1)} all-reduce(f32[4096]{0:T(1024)S(1)} %exponential_multiply_fusion.5), channel_id=1, replica_groups=mesh['row'=16,'col'=8] {'col'}, use_global_device_ids=true, to_apply=%region_15.15 | all-reduce | flops 4096 | bytes 32768 | tf_op jit(solution)/shard_map/cond/branch_1_fun/psum | solution.py:133
  290.4 39.0 %while.67 = (s32[]{:T(128)}, f32[4096]{0:T(1024)S(1)}, f32[4096]{0:T(1024)S(1)}, f32[8,512]{1,0:T(8,128)S(1)}, f32[8,512]{1,0:T(8,128)S(1)}, /*index=5*/f32[4096...) while((s32[]{:T(128)}, f32[4096]{0:T(1024)S(1)}, ...), condition=%wide.region_25.25_spmd, body=%wide.region_16.24_spmd.sunk | while | flops 553690112 | bytes 22839444 | solution.py:107
  329.4 72.4 %pmax.37 = f32[4096]{0:T(1024)S(1)} all-reduce(f32[4096]{0:T(1024)S(1)} %get-tuple-element.259), channel_id=1, replica_groups=mesh['row'=16,'col'=8] {'row'}, use_global_device_ids=true, to_apply=%region_26.26 | all-reduce | flops 4096 | bytes 32768 | tf_op jit(solution)/shard_map/cond/branch_1_fun/pmax | solution.py:139
  401.8 69.7 %psum.37 = f32[4096]{0:T(1024)S(1)} all-reduce(f32[4096]{0:T(1024)S(1)} %exponential_multiply_fusion.4), channel_id=1, replica_groups=mesh['row'=16,'col'=8] {'row'}, use_global_device_ids=true, to_apply=%region_27.27 | all-reduce | flops 4096 | bytes 32768 | tf_op jit(solution)/shard_map/cond/branch_1_fun/psum | solution.py:140
  471.6 47.9 %while.68 = (s32[]{:T(128)}, f32[8,512]{1,0:T(8,128)S(1)}, f32[8,512]{1,0:T(8,128)S(1)}, f32[4096]{0:T(1024)S(1)}, f32[8,512]{1,0:T(8,128)S(1)}, /*index=5*/f32[...) while((s32[]{:T(128)}, f32[8,512]{1,0:T(8,128)S(1)}, ...), condition=%wide.region_37.37_spmd, body=%wide.region_28.36_spmd.sunk | while | flops 553655808 | bytes 22722724 | solution.py:62
  471.6 1.7 fusion.176
  477.6 1.7 fusion.176
  483.6 1.7 fusion.176
  489.6 1.7 fusion.176
  495.6 1.7 fusion.176
  501.5 1.7 fusion.176
  507.5 1.7 fusion.176
  513.5 1.7 fusion.176
  519.5 23.6 %pmax.38 = f32[4096]{0:T(1024)S(1)} all-reduce(f32[4096]{0:T(1024)S(1)} %bitcast.301), channel_id=1, replica_groups=mesh['row'=16,'col'=8] {'col'}, use_global_device_ids=true, to_apply=%region_38.38 | all-reduce | flops 4096 | bytes 32768 | tf_op jit(solution)/shard_map/cond/branch_1_fun/pmax | solution.py:132
  543.1 23.6 %psum.38 = f32[4096]{0:T(1024)S(1)} all-reduce(f32[4096]{0:T(1024)S(1)} %exponential_multiply_fusion.3), channel_id=1, replica_groups=mesh['row'=16,'col'=8] {'col'}, use_global_device_ids=true, to_apply=%region_39.39 | all-reduce | flops 4096 | bytes 32768 | tf_op jit(solution)/shard_map/cond/branch_1_fun/psum | solution.py:133
  566.7 39.0 %while.69 = (s32[]{:T(128)}, f32[4096]{0:T(1024)S(1)}, f32[4096]{0:T(1024)S(1)}, f32[8,512]{1,0:T(8,128)S(1)}, f32[8,512]{1,0:T(8,128)S(1)}, /*index=5*/f32[4096...) while((s32[]{:T(128)}, f32[4096]{0:T(1024)S(1)}, ...), condition=%wide.region_49.49_spmd, body=%wide.region_40.48_spmd.sunk | while | flops 553690112 | bytes 22839444 | solution.py:107
  605.7 69.5 %pmax.39 = f32[4096]{0:T(1024)S(1)} all-reduce(f32[4096]{0:T(1024)S(1)} %get-tuple-element.263), channel_id=1, replica_groups=mesh['row'=16,'col'=8] {'row'}, use_global_device_ids=true, to_apply=%region_50.50 | all-reduce | flops 4096 | bytes 32768 | tf_op jit(solution)/shard_map/cond/branch_1_fun/pmax | solution.py:139
  675.2 69.7 %psum.39 = f32[4096]{0:T(1024)S(1)} all-reduce(f32[4096]{0:T(1024)S(1)} %exponential_multiply_fusion.2), channel_id=1, replica_groups=mesh['row'=16,'col'=8] {'row'}, use_global_device_ids=true, to_apply=%region_51.51 | all-reduce | flops 4096 | bytes 32768 | tf_op jit(solution)/shard_map/cond/branch_1_fun/psum | solution.py:140
  745.0 47.8 %while.70 = (s32[]{:T(128)}, f32[8,512]{1,0:T(8,128)S(1)}, f32[8,512]{1,0:T(8,128)S(1)}, f32[4096]{0:T(1024)S(1)}, f32[8,512]{1,0:T(8,128)S(1)}, /*index=5*/f32[...) while((s32[]{:T(128)}, f32[8,512]{1,0:T(8,128)S(1)}, ...), condition=%wide.region_61.61_spmd, body=%wide.region_52.60_spmd.sunk | while | flops 553655808 | bytes 22722724 | solution.py:62
  745.0 1.7 fusion.187
  751.0 1.7 fusion.187
  757.0 1.7 fusion.187
  763.0 1.7 fusion.187
  769.0 1.7 fusion.187
  774.9 1.7 fusion.187
  780.9 1.7 fusion.187
  786.9 1.7 fusion.187
  792.8 23.6 %pmax.40 = f32[4096]{0:T(1024)S(1)} all-reduce(f32[4096]{0:T(1024)S(1)} %bitcast.303), channel_id=1, replica_groups=mesh['row'=16,'col'=8] {'col'}, use_global_device_ids=true, to_apply=%region_62.62 | all-reduce | flops 4096 | bytes 32768 | tf_op jit(solution)/shard_map/cond/branch_1_fun/pmax | solution.py:132
  816.4 23.6 %psum.40 = f32[4096]{0:T(1024)S(1)} all-reduce(f32[4096]{0:T(1024)S(1)} %exponential_multiply_fusion.1), channel_id=1, replica_groups=mesh['row'=16,'col'=8] {'col'}, use_global_device_ids=true, to_apply=%region_63.63 | all-reduce | flops 4096 | bytes 32768 | tf_op jit(solution)/shard_map/cond/branch_1_fun/psum | solution.py:133
  840.6 39.1 %while.71 = (s32[]{:T(128)}, f32[4096]{0:T(1024)S(1)}, f32[4096]{0:T(1024)S(1)}, f32[8,512]{1,0:T(8,128)S(1)}, f32[8,512]{1,0:T(8,128)S(1)}, /*index=5*/f32[4096...) while((s32[]{:T(128)}, f32[4096]{0:T(1024)S(1)}, ...), condition=%wide.region_73.73_spmd, body=%wide.region_64.72_spmd.sunk | while | flops 553690112 | bytes 22839444 | solution.py:107
  879.7 69.6 %pmax.41 = f32[4096]{0:T(1024)S(1)} all-reduce(f32[4096]{0:T(1024)S(1)} %get-tuple-element.267), channel_id=1, replica_groups=mesh['row'=16,'col'=8] {'row'}, use_global_device_ids=true, to_apply=%region_74.74 | all-reduce | flops 4096 | bytes 32768 | tf_op jit(solution)/shard_map/cond/branch_1_fun/pmax | solution.py:139
  949.3 69.5 %psum.41 = f32[4096]{0:T(1024)S(1)} all-reduce(f32[4096]{0:T(1024)S(1)} %exponential_multiply_fusion), channel_id=1, replica_groups=mesh['row'=16,'col'=8] {'row'}, use_global_device_ids=true, to_apply=%region_75.75 | all-reduce | flops 4096 | bytes 32768 | tf_op jit(solution)/shard_map/cond/branch_1_fun/psum | solution.py:140
  (791 shorter events, 221.7 us)
Async XLA Ops:
  124.2 24.1 %all-gather.3.cloned.1.call-start = ((), (), s32[]{:S(2)}) async-start(), calls=%async_computation | async-start | bytes 1179648 | tf_op jit(solution)/shard_map/cond/branch_1_fun/all_gather | solution.py:120
  124.9 68.2 %all-gather.5.cloned.1.call-start = ((), (), s32[]{:S(2)}) async-start(), calls=%async_computation.1 | async-start | bytes 1114112 | tf_op jit(solution)/shard_map/cond/branch_1_fun/all_gather | solution.py:121
  148.3 46.7 %copy-start = (bf16[4096,128]{1,0:T(8,128)(2,1)S(1)}, bf16[4096,128]{1,0:T(8,128)(2,1)}, u32[]{:S(2)}) copy-start(bf16[4096,128]{1,0:T(8,128)(2,1)} %all-gather.3.cloned.1.call-done) | copy-start | bytes 3145732 | tf_op jit(solution)/shard_map/cond
  195.1 2.2 copy-start.1
  201.0 2.2 copy-start.1
  207.0 2.2 copy-start.1
  212.9 2.2 copy-start.1
  218.9 2.2 copy-start.1
  224.8 2.2 copy-start.1
  230.8 2.2 copy-start.1
  236.7 2.2 copy-start.1
  290.5 2.0 copy-start.2
  295.4 2.0 copy-start.2
  300.2 2.0 copy-start.2
  305.1 2.0 copy-start.2
  310.0 2.0 copy-start.2
  314.9 2.0 copy-start.2
  324.6 2.0 copy-start.2
  471.6 2.2 copy-start.3
  477.6 2.2 copy-start.3
  483.6 2.2 copy-start.3
  489.6 2.2 copy-start.3
  495.6 2.2 copy-start.3
  501.5 2.2 copy-start.3
  507.5 2.2 copy-start.3
  513.5 2.2 copy-start.3
  566.7 2.0 copy-start.4
  576.4 2.0 copy-start.4
  581.3 2.0 copy-start.4
  586.2 2.0 copy-start.4
  591.1 2.0 copy-start.4
  596.0 2.0 copy-start.4
  600.8 2.0 copy-start.4
  745.0 2.2 copy-start.5
  751.0 2.2 copy-start.5
  757.0 2.2 copy-start.5
  763.0 2.2 copy-start.5
  768.9 2.2 copy-start.5
  774.9 2.2 copy-start.5
  780.9 2.2 copy-start.5
  786.9 2.2 copy-start.5
  845.5 2.0 copy-start.6
  850.4 2.0 copy-start.6
  855.3 2.0 copy-start.6
  860.2 2.0 copy-start.6
  865.1 2.0 copy-start.6
  869.9 2.0 copy-start.6
  874.9 2.0 copy-start.6
  (5 other events, 8.4 us)
Sparse Core Ops, SparseCore 0:
  126.8 21.4 all-gather.2
  150.4 42.6 all-gather.4

commit v3 on v1

--- a/solution.py
+++ b/solution.py
@@ -13,6 +13,8 @@
 LOG2E = 1.0 / math.log(2.0)
 SCALE = 2.0 * LOG2E / EPS
 BACK = EPS / LOG2E
+FLOOR = 90.0
+CEIL = 100.0
 F32 = jnp.float32
 BF16 = jnp.bfloat16
 MESH = pl.DeviceIdType.MESH
@@ -28,12 +30,10 @@
     return high, mid, x - high - mid
 
 
-def pick3(x, index):
+def pick3(x, index, base, other):
     high, mid, low = split3(x)
-    zero = jnp.zeros_like(high)
-    return jnp.where(
-        index == 0, high, jnp.where(index == 1, mid, jnp.where(index == 2, low, zero))
-    ).astype(BF16)
+    found = jnp.where(index == base + 1, mid, jnp.where(index == base + 2, low, other))
+    return jnp.where(index == base, high, found).astype(BF16)
 
 
 def nt_dot(x, y):
@@ -41,6 +41,298 @@
 
 
 def kernel(
+    row_n, col_n, s_ref, t_ref, f_ref, g_ref,
+    s_all, t_all, s_ext, t_ext, kept, sums, highs, part, weight, s_sq, t_sq, shift_s, shift_t, from_col, from_row,
+    s_send, s_recv, t_send, t_recv, pair_send, pair_recv, col_send, col_recv, row_send, row_recv,
+):
+    own_s, depth = s_ref.shape
+    own_t = t_ref.shape[0]
+    ns, nt = own_s * col_n, own_t * row_n
+    total_s, total_t = float(ns * row_n), float(nt * col_n)
+    my_row, my_col = lax.axis_index("row"), lax.axis_index("col")
+    col_peers = [lax.rem(my_col + k, col_n) for k in range(1, col_n)]
+    row_peers = [lax.rem(my_row + k, row_n) for k in range(1, row_n)]
+    my_core = lax.rem(my_col, 2)
+    twin = my_col + 1 - 2 * my_core
+    chips = col_n // 2
+
+    barrier = pltpu.get_barrier_semaphore()
+    for peer in col_peers:
+        pl.semaphore_signal(barrier, inc=1, device_id={"col": peer}, device_id_type=MESH)
+    for peer in row_peers:
+        pl.semaphore_signal(barrier, inc=1, device_id={"row": peer}, device_id_type=MESH)
+
+    def s_block(index):
+        return pl.ds(pl.multiple_of(index * own_s, own_s), own_s)
+
+    def t_block(index):
+        return pl.ds(pl.multiple_of(index * own_t, own_t), own_t)
+
+    def s_from(k):
+        return lax.rem(my_col - 2 * k + col_n, col_n)
+
+    def twin_from(k):
+        return lax.rem(twin - 2 * k + col_n, col_n)
+
+    def t_from(k):
+        return lax.rem(my_row - k + row_n, row_n)
+
+    def t_copy(k):
+        return pltpu.make_async_remote_copy(
+            t_ref, t_all.at[t_block(my_row), :], t_send.at[k], t_recv.at[k],
+            device_id={"row": lax.rem(my_row + k, row_n)}, device_id_type=MESH,
+        )
+
+    def s_copy(k):
+        return pltpu.make_async_remote_copy(
+            s_ref, s_all.at[s_block(my_col), :], s_send.at[k], s_recv.at[k],
+            device_id={"col": lax.rem(my_col + 2 * k, col_n)}, device_id_type=MESH,
+        )
+
+    def twin_copy(k):
+        at = s_all.at[s_block(s_from(k)), :]
+        return pltpu.make_async_remote_copy(
+            s_ref if k == 0 else at, at, pair_send.at[k], pair_recv.at[k], device_id={"col": twin}, device_id_type=MESH
+        )
+
+    pl.semaphore_wait(barrier, col_n + row_n - 2)
+    for k in range(1, chips):
+        s_copy(k).start()
+    twin_copy(0).start()
+    for k in range(1, row_n):
+        t_copy(k).start()
+
+    chunk = 128
+
+    def ones_at(rows, first):
+        lane = lax.broadcasted_iota(jnp.int32, (rows, depth), 1)
+        return lane, jnp.where((lane >= first) & (lane < first + 3), 1.0, 0.0)
+
+    def spread(column):
+        return jnp.broadcast_to(column, (column.shape[0], depth))
+
+    def along_lanes(ext, first):
+        select = ones_at(16, first)[1].astype(BF16)
+        return nt_dot(select, ext[...])[0:1, :]
+
+    def t_prepare(index):
+        lane, ones = ones_at(own_t, 3)
+        for i in index:
+            x = t_all[t_block(i), :].astype(F32)
+            bias = spread(jnp.sum(x * x, axis=1, keepdims=True) * -0.5)
+            t_ext[t_block(i), :] = pick3(bias, lane, 0, ones)
+
+    def s_prepare(i):
+        lane, ones = ones_at(own_s, 0)
+        sample = jnp.concatenate([t_ref[...], t_ext[t_block(my_row), :]], axis=1)
+        x = jnp.concatenate([s_all[s_block(i), :], ones.astype(BF16)], axis=1)
+        shift = spread(-FLOOR / SCALE - jnp.max(nt_dot(x, sample), axis=1, keepdims=True))
+        s_ext[s_block(i), :] = pick3(shift, lane, 3, ones)
+
+    s_all[s_block(my_col), :] = s_ref[...]
+    t_all[t_block(my_row), :] = t_ref[...]
+    sums[...] = jnp.zeros_like(sums)
+    t_prepare([my_row])
+    s_prepare(my_col)
+
+    per = 2
+
+    def terms_with(t_index, s_index):
+        x = jnp.concatenate(
+            [jnp.concatenate([t_all[t_block(i), :], t_ext[t_block(i), :]], axis=1) for i in t_index], axis=0
+        )
+        high = None
+        for i in s_index:
+            at = s_block(i)
+            z = nt_dot(x, jnp.concatenate([s_all[at, :], s_ext[at, :]], axis=1))
+            for c in range(0, own_s, depth):
+                piece = z[:, c : c + depth]
+                high = piece if high is None else jnp.maximum(high, piece)
+            terms = jnp.exp2(z * SCALE).reshape(z.shape[0] // 8, 8, own_s)
+            sums[:, at] = sums[:, at] + jnp.sum(terms, axis=0)
+        for n, i in enumerate(t_index):
+            at = t_block(i)
+            highs[at, :] = jnp.maximum(highs[at, :], high[n * own_t : (n + 1) * own_t, :])
+
+    for k in range(1, chips):
+        s_copy(k).wait_recv()
+        twin_copy(k).start()
+        s_prepare(s_from(k))
+
+    for j in range(1, per):
+        t_copy(j).wait_recv()
+    t_prepare([t_from(j) for j in range(1, per)])
+    highs[...] = jnp.full_like(highs, -3e38)
+
+    def near(p, _):
+        terms_with([t_from(per * p + j) for j in range(per)], [s_from(k) for k in range(chips)])
+
+        @pl.when(p < row_n // per - 1)
+        def _():
+            following = [per * p + per + j for j in range(per)]
+            for k in following:
+                t_copy(k).wait_recv()
+            t_prepare([t_from(k) for k in following])
+
+        return 0
+
+    lax.fori_loop(0, row_n // per, near, 0)
+
+    for k in range(chips):
+        twin_copy(k).wait_recv()
+        s_prepare(twin_from(k))
+
+    def far(p, _):
+        terms_with([t_from(per * p + j) for j in range(per)], [twin_from(k) for k in range(chips)])
+        return 0
+
+    lax.fori_loop(0, row_n // per, far, 0)
+
+    for k in range(1, chips):
+        s_copy(k).wait_send()
+    for k in range(chips):
+        twin_copy(k).wait_send()
+    for k in range(1, row_n):
+        t_copy(k).wait_send()
+
+    def exchange(turn, sent, received, send, recv, axis, peers, meanwhile=None):
+        copies = [
+            pltpu.make_async_remote_copy(
+                sent, received.at[turn, k], send.at[turn, k], recv.at[turn, k],
+                device_id={axis: peer}, device_id_type=MESH,
+            )
+            for k, peer in enumerate(peers)
+        ]
+        for copy in copies:
+            copy.start()
+        if meanwhile is not None:
+            meanwhile()
+        for copy in copies:
+            copy.wait()
+        return [sent[...]] + [received[turn, k] for k in range(len(peers))]
+
+    def over_col(turn, meanwhile=None):
+        return exchange(turn, part.at[2 * turn], from_col, col_send, col_recv, "col", col_peers, meanwhile)
+
+    def over_row(turn, meanwhile=None):
+        return exchange(turn, part.at[2 * turn + 1], from_row, row_send, row_recv, "row", row_peers, meanwhile)
+
+    def s_norms():
+        ones = jnp.full((16, depth), 1.0, BF16)
+
+        def one(i, _):
+            rows = pl.ds(pl.multiple_of(i * own_s, own_s), own_s)
+            x = s_all[rows, :].astype(F32)
+            square = x * x
+            high = square.astype(BF16)
+            low = (square - high.astype(F32)).astype(BF16)
+            s_sq[:, rows] = (nt_dot(ones, high) + nt_dot(ones, low))[0:1, :]
+            return 0
+
+        lax.fori_loop(0, col_n, one, 0)
+
+    def combined_logs(logs):
+        highest = functools.reduce(jnp.maximum, logs)
+        return highest + log2(sum(jnp.exp2(x - highest) for x in logs))
+
+    def t_shift():
+        room = (FLOOR + math.log2(total_t) - CEIL) / SCALE
+
+        t_sq[...] = -2.0 * along_lanes(t_ext, 0)
+        size = min(512, nt)
+        lane, ones = ones_at(size, 0)
+
+        def one(i, _):
+            rows = pl.ds(pl.multiple_of(i * size, size), size)
+            bias = jnp.sum(jnp.where(lane < 3, t_ext[rows, :].astype(F32), 0.0), axis=1, keepdims=True)
+            shift = spread(bias - jnp.max(highs[rows, :], axis=1, keepdims=True) - room)
+            t_ext[rows, :] = pick3(shift, lane, 3, ones)
+            return 0
+
+        lax.fori_loop(0, nt // size, one, 0)
+        shift_t[...] = along_lanes(t_ext, 3)
+
+    shift_s[...] = along_lanes(s_ext, 3)
+    found = jnp.sum(sums[...], axis=0, keepdims=True)
+    logs = log2(found) - shift_s[...] * SCALE
+    part[0] = jnp.where(found < 2.0**120, logs, jnp.nan)
+    f_first = math.log2(total_t) - combined_logs(over_col(0, t_shift))
+    f_ref[...] = f_first
+
+    def s_bias(i, _):
+        size = min(512, ns)
+        lane, ones = ones_at(size, 3)
+        rows = pl.ds(pl.multiple_of(i * size, size), size)
+        bias = jnp.transpose(jnp.broadcast_to(f_ref[:, rows] * (1.0 / SCALE), (depth, size)))
+        s_ext[rows, :] = pick3(bias, lane, 0, ones)
+        return 0
+
+    lax.fori_loop(0, ns // min(512, ns), s_bias, 0)
+
+    width = min(512, nt)
+    step = min(2048, ns)
+
+    def second(i, _):
+        at = pl.ds(pl.multiple_of(i * width, width), width)
+        w = jnp.concatenate([t_all[at, :], t_ext[at, :]], axis=1)
+        summed = jnp.zeros((8, width), F32)
+        for q in range(ns // step):
+            rows = pl.ds(q * step, step)
+            terms = jnp.exp2(nt_dot(jnp.concatenate([s_all[rows, :], s_ext[rows, :]], axis=1), w) * SCALE)
+            kept[rows, at] = terms.astype(BF16)
+            summed = summed + jnp.sum(terms.reshape(step // 8, 8, width), axis=0)
+        part[1, :, at] = log2(jnp.sum(summed, axis=0, keepdims=True)) - shift_t[:, at] * SCALE
+        return 0
+
+    lax.fori_loop(0, nt // width, second, 0)
+    logs = combined_logs(over_row(0, s_norms))
+    held = logs + shift_t[...] * SCALE
+    g_first = jnp.where(held > -30.0, math.log2(total_s) - logs, jnp.nan)
+    g_ref[...] = g_first
+    weight[0] = jnp.exp2(g_first - shift_t[...] * SCALE)
+    weight[1] = weight[0]
+
+    def row_sums(out):
+        fine = chunk // 2
+
+        def one(i, _):
+            pieces = []
+            for h in range(0, chunk, fine):
+                rows = pl.ds(pl.multiple_of(i * chunk, chunk) + h, fine)
+                summed = jnp.zeros((fine, 128), F32)
+                for c in range(0, nt, 128):
+                    summed = summed + kept[rows, c : c + 128].astype(F32) * weight[1, :, c : c + 128]
+                pieces.append(summed)
+            turned = jnp.transpose(jnp.concatenate(pieces, axis=0))
+            out[:, pl.ds(pl.multiple_of(i * chunk, chunk), chunk)] = jnp.sum(turned, axis=0, keepdims=True)
+            return 0
+
+        lax.fori_loop(0, ns // chunk, one, 0)
+
+    def col_sums(x, out):
+        wide = min(2048, nt)
+        index = lax.broadcasted_iota(jnp.int32, (16, ns), 0)
+        lhs = pick3(jnp.broadcast_to(x, (16, ns)), index, 0, 0.0)
+
+        def one(i, _):
+            at = pl.ds(pl.multiple_of(i * wide, wide), wide)
+            got = jnp.dot(lhs, kept[:, at], preferred_element_type=F32)
+            out[:, at] = jnp.sum(got, axis=0, keepdims=True) * weight[0, :, at]
+            return 0
+
+        lax.fori_loop(0, nt // wide, one, 0)
+
+    for turn in range(1, ITERS):
+        row_sums(part.at[2 * turn])
+        u = total_t / sum(over_col(turn))
+        col_sums(u, part.at[2 * turn + 1])
+        v = total_s / sum(over_row(turn))
+        weight[1] = weight[0] * v
+    f_ref[...] = BACK * (f_ref[...] + log2(u)) + s_sq[...]
+    g_ref[...] = BACK * (g_ref[...] + log2(v)) + t_sq[...]
+
+
+def careful_kernel(
     row_n, col_n, s_ref, t_ref, f_ref, g_ref,
     s_all, t_all, s_ext, t_ext, kept, z0, z1, part, col_high, s_sq, t_sq, from_col, from_row,
     s_send, s_recv, t_send, t_recv, col_send, col_recv, row_send, row_recv,
@@ -100,7 +392,7 @@
         x = t_all[rows, :].astype(F32)
         t_sq[:, rows] = jnp.sum(jnp.transpose(x * x), axis=0, keepdims=True)
         bias = jnp.sum(x * x, axis=1, keepdims=True) * -0.5
-        t_ext[rows, :] = pick3(jnp.broadcast_to(bias, (chunk, depth)), lane)
+        t_ext[rows, :] = pick3(jnp.broadcast_to(bias, (chunk, depth)), lane, 0, 0.0)
         return 0
 
     lax.fori_loop(0, ns // chunk, s_prepare, 0)
@@ -193,7 +485,7 @@
     def s_bias(i, _):
         rows = pl.ds(pl.multiple_of(i * chunk, chunk), chunk)
         bias = jnp.transpose(jnp.broadcast_to(f_ref[:, rows] * (1.0 / SCALE), (depth, chunk)))
-        s_ext[rows, :] = pick3(bias, lane)
+        s_ext[rows, :] = pick3(bias, lane, 0, 0.0)
         return 0
 
     def t_ones(i, _):
@@ -210,7 +502,8 @@
     block = min(512, ns, nt)
 
     def parts_of(x):
-        return pick3(jnp.broadcast_to(x, (16, x.shape[1])), lax.broadcasted_iota(jnp.int32, (16, x.shape[1]), 0))
+        index = lax.broadcasted_iota(jnp.int32, (16, x.shape[1]), 0)
+        return pick3(jnp.broadcast_to(x, (16, x.shape[1])), index, 0, 0.0)
 
     def row_sums(x, out):
         lhs = parts_of(x)
@@ -244,7 +537,7 @@
     g_ref[...] = BACK * (g_ref[...] + log2(v)) + t_sq[...]
 
 
-def on_device(row_n, col_n, source, target):
+def careful(row_n, col_n, source, target):
     own_s, depth = source.shape
     own_t = target.shape[0]
     ns, nt = own_s * col_n, own_t * row_n
@@ -252,7 +545,7 @@
     vmem = pl.BlockSpec(memory_space=pltpu.VMEM)
     dma = pltpu.SemaphoreType.DMA
     f, g = pl.pallas_call(
-        functools.partial(kernel, row_n, col_n),
+        functools.partial(careful_kernel, row_n, col_n),
         out_shape=(jax.ShapeDtypeStruct((1, ns), F32), jax.ShapeDtypeStruct((1, nt), F32)),
         in_specs=[vmem, vmem],
         out_specs=(vmem, vmem),
@@ -280,13 +573,62 @@
             dma((ITERS, row_n - 1)),
         ],
         compiler_params=pltpu.CompilerParams(
+            collective_id=1, has_side_effects=True, vmem_limit_bytes=60 << 20
+        ),
+        cost_estimate=pl.CostEstimate(
+            flops=12 * ns * nt * depth, bytes_accessed=2 * (ns + nt) * depth, transcendentals=2 * ns * nt
+        ),
+    )(source, target)
+    return f.reshape(ns), g.reshape(nt)
+
+
+def on_device(row_n, col_n, source, target):
+    own_s, depth = source.shape
+    own_t = target.shape[0]
+    ns, nt = own_s * col_n, own_t * row_n
+    vmem = pl.BlockSpec(memory_space=pltpu.VMEM)
+    dma = pltpu.SemaphoreType.DMA
+    f, g = pl.pallas_call(
+        functools.partial(kernel, row_n, col_n),
+        out_shape=(jax.ShapeDtypeStruct((1, ns), F32), jax.ShapeDtypeStruct((1, nt), F32)),
+        in_specs=[vmem, vmem],
+        out_specs=(vmem, vmem),
+        scratch_shapes=[
+            pltpu.VMEM((ns, depth), BF16),
+            pltpu.VMEM((nt, depth), BF16),
+            pltpu.VMEM((ns, depth), BF16),
+            pltpu.VMEM((nt, depth), BF16),
+            pltpu.VMEM((ns, nt), BF16),
+            pltpu.VMEM((8, ns), F32),
+            pltpu.VMEM((nt, depth), F32),
+            pltpu.VMEM((2 * ITERS, 1, max(ns, nt)), F32),
+            pltpu.VMEM((2, 1, nt), F32),
+            pltpu.VMEM((1, ns), F32),
+            pltpu.VMEM((1, nt), F32),
+            pltpu.VMEM((1, ns), F32),
+            pltpu.VMEM((1, nt), F32),
+            pltpu.VMEM((ITERS, col_n - 1, 1, ns), F32),
+            pltpu.VMEM((ITERS, row_n - 1, 1, nt), F32),
+            dma((col_n // 2,)),
+            dma((col_n // 2,)),
+            dma((row_n,)),
+            dma((row_n,)),
+            dma((col_n // 2,)),
+            dma((col_n // 2,)),
+            dma((ITERS, col_n - 1)),
+            dma((ITERS, col_n - 1)),
+            dma((ITERS, row_n - 1)),
+            dma((ITERS, row_n - 1)),
+        ],
+        compiler_params=pltpu.CompilerParams(
             collective_id=0, has_side_effects=True, vmem_limit_bytes=60 << 20
         ),
         cost_estimate=pl.CostEstimate(
             flops=12 * ns * nt * depth, bytes_accessed=2 * (ns + nt) * depth, transcendentals=2 * ns * nt
         ),
     )(source, target)
-    return f.reshape(ns), g.reshape(nt)
+    fast = f.reshape(ns), g.reshape(nt)
+    return lax.cond(jnp.isnan(f[0, 0]), lambda: careful(row_n, col_n, source, target), lambda: fast)
 
 
 def solution(mesh):

time: 136 us -> 237 us (1.74)
  Pallas kernels: 132 us -> 232 us
    pallas_call x0 -> x1, Pallas kernels: none -> 126 us  [careful(): pl.pallas_call(functools.partial(careful_kernel, row_n, col_n), out_shape...]
    pallas_call x1, Pallas kernels: 132 us -> 106 us  [on_device(): pl.pallas_call(functools.partial(kernel, row_n, col_n), out_shape=(jax.Sh...]
where the time goes in v3:
time: 237 us; the launch traced here: 236 us
  Pallas kernels  232 us (98%)
    pallas_call x1, Pallas kernels, careful(): pl.pallas_call(functools.partial(careful_kernel, row_n, col_n), out_shape...  126 us
    pallas_call x1, Pallas kernels, on_device(): pl.pallas_call(functools.partial(kernel, row_n, col_n), out_shape=(jax.Sh...  106 us

profile of v3, /device:TPU:0, one launch (start us, length us, event | category | flops | bytes accessed | tf_op | source)
XLA Modules:
  0.0 236.0 jit_solution(16763063163274351677)
XLA Ops:
  0.6 0.0 copy-start
  0.6 0.0 copy-start.1
  0.6 105.6 %shard_map.41 = (f32[1,4096]{1,0:T(1,128)S(1)}, f32[1,4096]{1,0:T(1,128)S(1)}) custom-call(bf16[512,128]{1,0:T(8,128)(2,1)} %s_ref.1, bf16[256,128]{1,0:T(8,128)(2,1)} %t_ref.1), custom_call_target="tpu_custom_call" | custom-call | flops 25769803776 | bytes 2097152 | tf_op jit(solution)/shard_map/pallas_call | solution.py:591
  106.3 0.5 slice.3
  108.1 0.0 copy-done
  108.1 0.0 copy-done.1
  108.1 126.6 %conditional.1 = (f32[4096]{0:T(1024)S(1)}, f32[4096]{0:T(1024)S(1)}) conditional(s32[]{:T(128)} %bitcast.4, (f32[1,4096]{1,0:T(1,128)S(1)}, f32[1,4096]{1,0:T(1,128)S(1)}) %shard_map.41, (bf16[512,128]{1,0:T(8,128)(2,1)S(1)}, bf16[256,128]{1,0:T(8,128)(2,1)S(1)}) %tuple.29), branch_computations={%region_0.0_spmd, %region_1.0_spmd} | conditional | flops 25769803776 | bytes 2097168 | solution.py:631
  108.3 126.4 %branch_1_fun.1 = (f32[1,4096]{1,0:T(1,128)S(1)}, f32[1,4096]{1,0:T(1,128)S(1)}) custom-call(bf16[512,128]{1,0:T(8,128)(2,1)S(1)} %get-tuple-element.14.s_ref, bf16[256,128]{1,0:T(8,128)(2,1)S(1)} %get-tuple-element.15.t_ref), custom_call_target="tpu_custom_call" | custom-call | flops 25769803776 | bytes 2097152 | tf_op jit(solution)/shard_map/cond/branch_1_fun/pallas_call | solution.py:547
  234.7 0.6 copy.12
  235.3 0.6 copy.13
Async XLA Ops:
  0.6 107.5 %copy-start = (bf16[512,128]{1,0:T(8,128)(2,1)S(1)}, bf16[512,128]{1,0:T(8,128)(2,1)}, u32[]{:S(2)}) copy-start(bf16[512,128]{1,0:T(8,128)(2,1)} %s_ref.1) | copy-start | bytes 393220
  0.6 107.5 %copy-start.1 = (bf16[256,128]{1,0:T(8,128)(2,1)S(1)}, bf16[256,128]{1,0:T(8,128)(2,1)}, u32[]{:S(2)}) copy-start(bf16[256,128]{1,0:T(8,128)(2,1)} %t_ref.1) | copy-start | bytes 196612

commit v4 on v3

--- a/solution.py
+++ b/solution.py
@@ -42,7 +42,8 @@
 
 def kernel(
     row_n, col_n, s_ref, t_ref, f_ref, g_ref,
-    s_all, t_all, s_ext, t_ext, kept, sums, highs, part, weight, s_sq, t_sq, shift_s, shift_t, from_col, from_row,
+    s_all, t_all, s_ext, t_ext, kept, sums, sums_t, highs, row_part, col_part, part, weight, s_sq, t_sq, shift_s, shift_t,
+    from_col, from_row,
     s_send, s_recv, t_send, t_recv, pair_send, pair_recv, col_send, col_recv, row_send, row_recv,
 ):
     own_s, depth = s_ref.shape
@@ -113,7 +114,7 @@
 
     def along_lanes(ext, first):
         select = ones_at(16, first)[1].astype(BF16)
-        return nt_dot(select, ext[...])[0:1, :]
+        return nt_dot(select, ext)[0:1, :]
 
     def t_prepare(index):
         lane, ones = ones_at(own_t, 3)
@@ -136,14 +137,22 @@
     s_prepare(my_col)
 
     per = 2
-
-    def terms_with(t_index, s_index):
+    half_s, half_t = ns // 2, nt // 2
+    halves = (0, 1)
+
+    def s_half(h):
+        return pl.ds(h * half_s, half_s)
+
+    def t_half(h):
+        return pl.ds(h * half_t, half_t)
+
+    def terms_with(t_index, h):
         x = jnp.concatenate(
             [jnp.concatenate([t_all[t_block(i), :], t_ext[t_block(i), :]], axis=1) for i in t_index], axis=0
         )
         high = None
-        for i in s_index:
-            at = s_block(i)
+        for i in range(h * col_n // 2, (h + 1) * col_n // 2):
+            at = pl.ds(i * own_s, own_s)
             z = nt_dot(x, jnp.concatenate([s_all[at, :], s_ext[at, :]], axis=1))
             for c in range(0, own_s, depth):
                 piece = z[:, c : c + depth]
@@ -154,18 +163,56 @@
             at = t_block(i)
             highs[at, :] = jnp.maximum(highs[at, :], high[n * own_t : (n + 1) * own_t, :])
 
+    def over(axis, turn, h):
+        if axis == "col":
+            here, there, send, recv, peers, at = part.at[2 * turn], from_col, col_send, col_recv, col_peers, s_half(h)
+        else:
+            here, there, send, recv, peers, at = part.at[2 * turn + 1], from_row, row_send, row_recv, row_peers, t_half(h)
+        return [
+            pltpu.make_async_remote_copy(
+                here.at[:, at], there.at[turn, k, :, at], send.at[turn, h, k], recv.at[turn, h, k],
+                device_id={axis: peer}, device_id_type=MESH,
+            )
+            for k, peer in enumerate(peers)
+        ]
+
+    def start(axis, turn, h):
+        for copy in over(axis, turn, h):
+            copy.start()
+
+    def finish(axis, turn, h):
+        for copy in over(axis, turn, h):
+            copy.wait()
+        if axis == "col":
+            return [part[2 * turn, :, s_half(h)]] + [from_col[turn, k, :, s_half(h)] for k in range(col_n - 1)]
+        return [part[2 * turn + 1, :, t_half(h)]] + [from_row[turn, k, :, t_half(h)] for k in range(row_n - 1)]
+
+    def combined_logs(logs):
+        highest = functools.reduce(jnp.maximum, logs)
+        return highest + log2(sum(jnp.exp2(x - highest) for x in logs))
+
+    def send_logs(h):
+        at = s_half(h)
+        shift_s[:, at] = along_lanes(s_ext[at, :], 3)
+        found = jnp.sum(sums[:, at], axis=0, keepdims=True)
+        logs = log2(found) - shift_s[:, at] * SCALE
+        part[0, :, at] = jnp.where(found < 2.0**120, logs, jnp.nan)
+        start("col", 0, h)
+
     for k in range(1, chips):
         s_copy(k).wait_recv()
         twin_copy(k).start()
         s_prepare(s_from(k))
-
     for j in range(1, per):
         t_copy(j).wait_recv()
     t_prepare([t_from(j) for j in range(1, per)])
     highs[...] = jnp.full_like(highs, -3e38)
-
-    def near(p, _):
-        terms_with([t_from(per * p + j) for j in range(per)], [s_from(k) for k in range(chips)])
+    for k in range(chips):
+        twin_copy(k).wait_recv()
+        s_prepare(twin_from(k))
+
+    def early(p, _):
+        terms_with([t_from(per * p + j) for j in range(per)], 0)
 
         @pl.when(p < row_n // per - 1)
         def _():
@@ -176,17 +223,14 @@
 
         return 0
 
-    lax.fori_loop(0, row_n // per, near, 0)
-
-    for k in range(chips):
-        twin_copy(k).wait_recv()
-        s_prepare(twin_from(k))
-
-    def far(p, _):
-        terms_with([t_from(per * p + j) for j in range(per)], [twin_from(k) for k in range(chips)])
-        return 0
-
-    lax.fori_loop(0, row_n // per, far, 0)
+    def late(p, _):
+        terms_with([t_from(per * p + j) for j in range(per)], 1)
+        return 0
+
+    lax.fori_loop(0, row_n // per, early, 0)
+    send_logs(0)
+    lax.fori_loop(0, row_n // per, late, 0)
+    send_logs(1)
 
     for k in range(1, chips):
         s_copy(k).wait_send()
@@ -195,141 +239,139 @@
     for k in range(1, row_n):
         t_copy(k).wait_send()
 
-    def exchange(turn, sent, received, send, recv, axis, peers, meanwhile=None):
-        copies = [
-            pltpu.make_async_remote_copy(
-                sent, received.at[turn, k], send.at[turn, k], recv.at[turn, k],
-                device_id={axis: peer}, device_id_type=MESH,
-            )
-            for k, peer in enumerate(peers)
-        ]
-        for copy in copies:
-            copy.start()
-        if meanwhile is not None:
-            meanwhile()
-        for copy in copies:
-            copy.wait()
-        return [sent[...]] + [received[turn, k] for k in range(len(peers))]
-
-    def over_col(turn, meanwhile=None):
-        return exchange(turn, part.at[2 * turn], from_col, col_send, col_recv, "col", col_peers, meanwhile)
-
-    def over_row(turn, meanwhile=None):
-        return exchange(turn, part.at[2 * turn + 1], from_row, row_send, row_recv, "row", row_peers, meanwhile)
-
-    def s_norms():
-        ones = jnp.full((16, depth), 1.0, BF16)
-
-        def one(i, _):
-            rows = pl.ds(pl.multiple_of(i * own_s, own_s), own_s)
-            x = s_all[rows, :].astype(F32)
-            square = x * x
-            high = square.astype(BF16)
-            low = (square - high.astype(F32)).astype(BF16)
-            s_sq[:, rows] = (nt_dot(ones, high) + nt_dot(ones, low))[0:1, :]
-            return 0
-
-        lax.fori_loop(0, col_n, one, 0)
-
-    def combined_logs(logs):
-        highest = functools.reduce(jnp.maximum, logs)
-        return highest + log2(sum(jnp.exp2(x - highest) for x in logs))
-
-    def t_shift():
-        room = (FLOOR + math.log2(total_t) - CEIL) / SCALE
-
-        t_sq[...] = -2.0 * along_lanes(t_ext, 0)
+    room = (FLOOR + math.log2(total_t) - CEIL) / SCALE
+
+    def t_shift(i, _):
         size = min(512, nt)
         lane, ones = ones_at(size, 0)
-
+        rows = pl.ds(pl.multiple_of(i * size, size), size)
+        bias = jnp.sum(jnp.where(lane < 3, t_ext[rows, :].astype(F32), 0.0), axis=1, keepdims=True)
+        shift = spread(bias - jnp.max(highs[rows, :], axis=1, keepdims=True) - room)
+        t_ext[rows, :] = pick3(shift, lane, 3, ones)
+        return 0
+
+    t_sq[...] = -2.0 * along_lanes(t_ext[...], 0)
+    lax.fori_loop(0, nt // min(512, nt), t_shift, 0)
+    shift_t[...] = along_lanes(t_ext[...], 3)
+
+    width = min(512, half_t)
+
+    def second(h):
         def one(i, _):
-            rows = pl.ds(pl.multiple_of(i * size, size), size)
-            bias = jnp.sum(jnp.where(lane < 3, t_ext[rows, :].astype(F32), 0.0), axis=1, keepdims=True)
-            shift = spread(bias - jnp.max(highs[rows, :], axis=1, keepdims=True) - room)
-            t_ext[rows, :] = pick3(shift, lane, 3, ones)
+            at = pl.ds(pl.multiple_of(i * width, width), width)
+            rows = s_half(h)
+            x = jnp.concatenate([s_all[rows, :], s_ext[rows, :]], axis=1)
+            w = jnp.concatenate([t_all[at, :], t_ext[at, :]], axis=1)
+            terms = jnp.exp2(nt_dot(x, w) * SCALE)
+            kept[rows, at] = terms.astype(BF16)
+            summed = jnp.sum(terms.reshape(half_s // 8, 8, width), axis=0)
+            if h == 0:
+                sums_t[:, at] = summed
+            else:
+                summed = jnp.sum(summed + sums_t[:, at], axis=0, keepdims=True)
+                part[1, :, at] = log2(summed) - shift_t[:, at] * SCALE
             return 0
 
-        lax.fori_loop(0, nt // size, one, 0)
-        shift_t[...] = along_lanes(t_ext, 3)
-
-    shift_s[...] = along_lanes(s_ext, 3)
-    found = jnp.sum(sums[...], axis=0, keepdims=True)
-    logs = log2(found) - shift_s[...] * SCALE
-    part[0] = jnp.where(found < 2.0**120, logs, jnp.nan)
-    f_first = math.log2(total_t) - combined_logs(over_col(0, t_shift))
-    f_ref[...] = f_first
-
-    def s_bias(i, _):
-        size = min(512, ns)
-        lane, ones = ones_at(size, 3)
-        rows = pl.ds(pl.multiple_of(i * size, size), size)
-        bias = jnp.transpose(jnp.broadcast_to(f_ref[:, rows] * (1.0 / SCALE), (depth, size)))
-        s_ext[rows, :] = pick3(bias, lane, 0, ones)
-        return 0
-
-    lax.fori_loop(0, ns // min(512, ns), s_bias, 0)
-
-    width = min(512, nt)
-    step = min(2048, ns)
-
-    def second(i, _):
-        at = pl.ds(pl.multiple_of(i * width, width), width)
-        w = jnp.concatenate([t_all[at, :], t_ext[at, :]], axis=1)
-        summed = jnp.zeros((8, width), F32)
-        for q in range(ns // step):
-            rows = pl.ds(q * step, step)
-            terms = jnp.exp2(nt_dot(jnp.concatenate([s_all[rows, :], s_ext[rows, :]], axis=1), w) * SCALE)
-            kept[rows, at] = terms.astype(BF16)
-            summed = summed + jnp.sum(terms.reshape(step // 8, 8, width), axis=0)
-        part[1, :, at] = log2(jnp.sum(summed, axis=0, keepdims=True)) - shift_t[:, at] * SCALE
-        return 0
-
-    lax.fori_loop(0, nt // width, second, 0)
-    logs = combined_logs(over_row(0, s_norms))
-    held = logs + shift_t[...] * SCALE
-    g_first = jnp.where(held > -30.0, math.log2(total_s) - logs, jnp.nan)
-    g_ref[...] = g_first
-    weight[0] = jnp.exp2(g_first - shift_t[...] * SCALE)
-    weight[1] = weight[0]
-
-    def row_sums(out):
-        fine = chunk // 2
-
+        return one
+
+    for h in halves:
+        at = s_half(h)
+        f_ref[:, at] = math.log2(total_t) - combined_logs(finish("col", 0, h))
+
+        def s_bias(i, _):
+            size = min(512, half_s)
+            lane, ones = ones_at(size, 3)
+            rows = pl.ds(pl.multiple_of(i * size + h * half_s, size), size)
+            bias = jnp.transpose(jnp.broadcast_to(f_ref[:, rows] * (1.0 / SCALE), (depth, size)))
+            s_ext[rows, :] = pick3(bias, lane, 0, ones)
+            return 0
+
+        lax.fori_loop(0, half_s // min(512, half_s), s_bias, 0)
+        if h == 0:
+            lax.fori_loop(0, nt // width, second(h), 0)
+    for h in halves:
+        lax.fori_loop(h * half_t // width, (h + 1) * half_t // width, second(1), 0)
+        start("row", 0, h)
+
+    def s_norms(i, _):
+        ones = jnp.full((16, depth), 1.0, BF16)
+        rows = pl.ds(pl.multiple_of(i * own_s, own_s), own_s)
+        x = s_all[rows, :].astype(F32)
+        square = x * x
+        high = square.astype(BF16)
+        low = (square - high.astype(F32)).astype(BF16)
+        s_sq[:, rows] = (nt_dot(ones, high) + nt_dot(ones, low))[0:1, :]
+        return 0
+
+    lax.fori_loop(0, col_n, s_norms, 0)
+
+    size = min(512, half_s)
+    fine = min(64, size)
+
+    def row_sums(h, out):
         def one(i, _):
-            pieces = []
-            for h in range(0, chunk, fine):
-                rows = pl.ds(pl.multiple_of(i * chunk, chunk) + h, fine)
-                summed = jnp.zeros((fine, 128), F32)
-                for c in range(0, nt, 128):
-                    summed = summed + kept[rows, c : c + 128].astype(F32) * weight[1, :, c : c + 128]
-                pieces.append(summed)
-            turned = jnp.transpose(jnp.concatenate(pieces, axis=0))
-            out[:, pl.ds(pl.multiple_of(i * chunk, chunk), chunk)] = jnp.sum(turned, axis=0, keepdims=True)
+            for q in range(0, size, 128):
+                pieces = []
+                for r in range(q, q + 128, fine):
+                    rows = pl.ds(pl.multiple_of(i * size, size) + r, fine)
+                    summed = jnp.zeros((fine, 128), F32) if out is None else row_part[rows, :]
+                    for c in range(h * half_t, (h + 1) * half_t, 128):
+                        summed = summed + kept[rows, c : c + 128].astype(F32) * weight[1, :, c : c + 128]
+                    if out is None:
+                        row_part[rows, :] = summed
+                    pieces.append(summed)
+                if out is not None:
+                    turned = jnp.transpose(jnp.concatenate(pieces, axis=0))
+                    at = pl.ds(pl.multiple_of(i * size, size) + q, 128)
+                    out[:, at] = jnp.sum(turned, axis=0, keepdims=True)
             return 0
 
-        lax.fori_loop(0, ns // chunk, one, 0)
-
-    def col_sums(x, out):
-        wide = min(2048, nt)
-        index = lax.broadcasted_iota(jnp.int32, (16, ns), 0)
-        lhs = pick3(jnp.broadcast_to(x, (16, ns)), index, 0, 0.0)
-
-        def one(i, _):
-            at = pl.ds(pl.multiple_of(i * wide, wide), wide)
-            got = jnp.dot(lhs, kept[:, at], preferred_element_type=F32)
-            out[:, at] = jnp.sum(got, axis=0, keepdims=True) * weight[0, :, at]
-            return 0
-
-        lax.fori_loop(0, nt // wide, one, 0)
-
-    for turn in range(1, ITERS):
-        row_sums(part.at[2 * turn])
-        u = total_t / sum(over_col(turn))
-        col_sums(u, part.at[2 * turn + 1])
-        v = total_s / sum(over_row(turn))
-        weight[1] = weight[0] * v
-    f_ref[...] = BACK * (f_ref[...] + log2(u)) + s_sq[...]
-    g_ref[...] = BACK * (g_ref[...] + log2(v)) + t_sq[...]
+        return one
+
+    def col_sums(lhs, h, at):
+        got = jnp.dot(lhs, kept[s_half(h), at], preferred_element_type=F32)
+        return jnp.sum(got, axis=0, keepdims=True)
+
+    def lhs_of(x):
+        index = lax.broadcasted_iota(jnp.int32, (16, half_s), 0)
+        return pick3(jnp.broadcast_to(x, (16, half_s)), index, 0, 0.0)
+
+    for turn in range(1, ITERS + 1):
+        for h in halves:
+            at = t_half(h)
+            arrived = finish("row", turn - 1, h)
+            if turn == 1:
+                logs = combined_logs(arrived)
+                held = logs + shift_t[:, at] * SCALE
+                g_ref[:, at] = jnp.where(held > -30.0, math.log2(total_s) - logs, jnp.nan)
+                weight[0, :, at] = jnp.exp2(g_ref[:, at] - shift_t[:, at] * SCALE)
+                weight[1, :, at] = weight[0, :, at]
+            else:
+                v = total_s / sum(arrived)
+                if turn < ITERS:
+                    weight[1, :, at] = weight[0, :, at] * v
+                else:
+                    g_ref[:, at] = BACK * (g_ref[:, at] + log2(v)) + t_sq[:, at]
+            if turn < ITERS and h == 0:
+                lax.fori_loop(0, ns // size, row_sums(0, None), 0)
+        if turn == ITERS:
+            break
+        for h in halves:
+            lax.fori_loop(h * half_s // size, (h + 1) * half_s // size, row_sums(1, part.at[2 * turn]), 0)
+            start("col", turn, h)
+        for h in halves:
+            u = total_t / sum(finish("col", turn, h))
+            if turn == ITERS - 1:
+                f_ref[:, s_half(h)] = BACK * (f_ref[:, s_half(h)] + log2(u)) + s_sq[:, s_half(h)]
+            lhs = lhs_of(u)
+            for c in halves:
+                at = t_half(c)
+                got = col_sums(lhs, h, at)
+                if h == 0:
+                    col_part[:, at] = got
+                else:
+                    part[2 * turn + 1, :, at] = (got + col_part[:, at]) * weight[0, :, at]
+                    start("row", turn, c)
 
 
 def careful_kernel(
@@ -600,7 +642,10 @@
             pltpu.VMEM((nt, depth), BF16),
             pltpu.VMEM((ns, nt), BF16),
             pltpu.VMEM((8, ns), F32),
+            pltpu.VMEM((8, nt), F32),
             pltpu.VMEM((nt, depth), F32),
+            pltpu.VMEM((ns, 128), F32),
+            pltpu.VMEM((1, nt), F32),
             pltpu.VMEM((2 * ITERS, 1, max(ns, nt)), F32),
             pltpu.VMEM((2, 1, nt), F32),
             pltpu.VMEM((1, ns), F32),
@@ -615,10 +660,10 @@
             dma((row_n,)),
             dma((col_n // 2,)),
             dma((col_n // 2,)),
-            dma((ITERS, col_n - 1)),
-            dma((ITERS, col_n - 1)),
-            dma((ITERS, row_n - 1)),
-            dma((ITERS, row_n - 1)),
+            dma((ITERS, 2, col_n - 1)),
+            dma((ITERS, 2, col_n - 1)),
+            dma((ITERS, 2, row_n - 1)),
+            dma((ITERS, 2, row_n - 1)),
         ],
         compiler_params=pltpu.CompilerParams(
             collective_id=0, has_side_effects=True, vmem_limit_bytes=60 << 20

time: 237 us -> 221 us (0.932)
  Pallas kernels: 232 us -> 217 us
    pallas_call x1, Pallas kernels: 106 us -> 91.1 us  [on_device(): pl.pallas_call(functools.partial(kernel, row_n, col_n), out_shape=(jax.Sh...]
where the time goes in v4:
time: 221 us
  Pallas kernels  217 us (98%)
    pallas_call x1, Pallas kernels, careful(): pl.pallas_call(functools.partial(careful_kernel, row_n, col_n), out_shape...  126 us
    pallas_call x1, Pallas kernels, on_device(): pl.pallas_call(functools.partial(kernel, row_n, col_n), out_shape=(jax.Sh...  91.1 us

profile of v4, /device:TPU:0, one launch (start us, length us, event | category | flops | bytes accessed | tf_op | source)
XLA Modules:
  0.0 220.7 jit_solution(5070689709833156426)
XLA Ops:
  0.6 0.0 copy-start
  0.6 0.0 copy-start.1
  0.6 91.1 %shard_map.41 = (f32[1,4096]{1,0:T(1,128)S(1)}, f32[1,4096]{1,0:T(1,128)S(1)}) custom-call(bf16[512,128]{1,0:T(8,128)(2,1)} %s_ref.1, bf16[256,128]{1,0:T(8,128)(2,1)} %t_ref.1), custom_call_target="tpu_custom_call" | custom-call | flops 25769803776 | bytes 2097152 | tf_op jit(solution)/shard_map/pallas_call | solution.py:633
  91.8 0.5 slice.3
  93.6 0.0 copy-done
  93.6 0.0 copy-done.1
  93.6 125.8 %conditional.1 = (f32[4096]{0:T(1024)S(1)}, f32[4096]{0:T(1024)S(1)}) conditional(s32[]{:T(128)} %bitcast.4, (f32[1,4096]{1,0:T(1,128)S(1)}, f32[1,4096]{1,0:T(1,128)S(1)}) %shard_map.41, (bf16[512,128]{1,0:T(8,128)(2,1)S(1)}, bf16[256,128]{1,0:T(8,128)(2,1)S(1)}) %tuple.29), branch_computations={%region_0.0_spmd, %region_1.0_spmd} | conditional | flops 25769803776 | bytes 2097168 | solution.py:676
  93.6 125.8 %branch_1_fun.1 = (f32[1,4096]{1,0:T(1,128)S(1)}, f32[1,4096]{1,0:T(1,128)S(1)}) custom-call(bf16[512,128]{1,0:T(8,128)(2,1)S(1)} %get-tuple-element.14.s_ref, bf16[256,128]{1,0:T(8,128)(2,1)S(1)} %get-tuple-element.15.t_ref), custom_call_target="tpu_custom_call" | custom-call | flops 25769803776 | bytes 2097152 | tf_op jit(solution)/shard_map/cond/branch_1_fun/pallas_call | solution.py:589
  219.5 0.6 copy.12
  220.1 0.6 copy.13
Async XLA Ops:
  0.6 93.0 %copy-start = (bf16[512,128]{1,0:T(8,128)(2,1)S(1)}, bf16[512,128]{1,0:T(8,128)(2,1)}, u32[]{:S(2)}) copy-start(bf16[512,128]{1,0:T(8,128)(2,1)} %s_ref.1) | copy-start | bytes 393220
  0.6 93.0 %copy-start.1 = (bf16[256,128]{1,0:T(8,128)(2,1)S(1)}, bf16[256,128]{1,0:T(8,128)(2,1)}, u32[]{:S(2)}) copy-start(bf16[256,128]{1,0:T(8,128)(2,1)} %t_ref.1) | copy-start | bytes 196612

commit v5 on v4

--- a/solution.py
+++ b/solution.py
@@ -75,13 +75,27 @@
     def twin_from(k):
         return lax.rem(twin - 2 * k + col_n, col_n)
 
+    side = math.isqrt(row_n)
+    my_z, my_x = my_row // side, my_row % side
+
+    def away(k):
+        z, x = 2 * (k // 8) + (k // 2) % 2, 2 * ((k // 4) % 2) + k % 2
+        return z + z // 2 - 2 * (z // 3), x + x // 2 - 2 * (x // 3)
+
     def t_from(k):
-        return lax.rem(my_row - k + row_n, row_n)
+        z, x = away(k)
+        return (my_z - z + side) % side * side + (my_x - x + side) % side
+
+    def t_to(k):
+        z, x = away(k)
+        return (my_z + z) % side * side + (my_x + x) % side
+
+    waves = [[k for k in wave if k < row_n] for wave in ((1, 2, 3, 4, 8), (5, 6, 7, 9, 10), (11, 12, 13, 14, 15))]
 
     def t_copy(k):
         return pltpu.make_async_remote_copy(
             t_ref, t_all.at[t_block(my_row), :], t_send.at[k], t_recv.at[k],
-            device_id={"row": lax.rem(my_row + k, row_n)}, device_id_type=MESH,
+            device_id={"row": t_to(k)}, device_id_type=MESH,
         )
 
     def s_copy(k):
@@ -100,7 +114,7 @@
     for k in range(1, chips):
         s_copy(k).start()
     twin_copy(0).start()
-    for k in range(1, row_n):
+    for k in waves[0]:
         t_copy(k).start()
 
     chunk = 128
@@ -199,14 +213,20 @@
         part[0, :, at] = jnp.where(found < 2.0**120, logs, jnp.nan)
         start("col", 0, h)
 
+    for before, wave in zip(waves, waves[1:]):
+        for k in before:
+            t_copy(k).wait_send()
+        for k in wave:
+            t_copy(k).start()
+        if before is waves[0]:
+            for j in range(1, per):
+                t_copy(j).wait_recv()
+            t_prepare([t_from(j) for j in range(1, per)])
+            highs[...] = jnp.full_like(highs, -3e38)
     for k in range(1, chips):
         s_copy(k).wait_recv()
         twin_copy(k).start()
         s_prepare(s_from(k))
-    for j in range(1, per):
-        t_copy(j).wait_recv()
-    t_prepare([t_from(j) for j in range(1, per)])
-    highs[...] = jnp.full_like(highs, -3e38)
     for k in range(chips):
         twin_copy(k).wait_recv()
         s_prepare(twin_from(k))
@@ -236,7 +256,7 @@
         s_copy(k).wait_send()
     for k in range(chips):
         twin_copy(k).wait_send()
-    for k in range(1, row_n):
+    for k in waves[2]:
         t_copy(k).wait_send()
 
     room = (FLOOR + math.log2(total_t) - CEIL) / SCALE

time: 221 us -> 223 us (level)
  no operation moved by 1% of the time
where the time goes in v5:
time: 223 us
  Pallas kernels  219 us (98%)
    pallas_call x1, Pallas kernels, careful(): pl.pallas_call(functools.partial(careful_kernel, row_n, col_n), out_shape...  126 us
    pallas_call x1, Pallas kernels, on_device(): pl.pallas_call(functools.partial(kernel, row_n, col_n), out_shape=(jax.Sh...  92.9 us

profile of v5, /device:TPU:0, one launch (start us, length us, event | category | flops | bytes accessed | tf_op | source)
XLA Modules:
  0.0 222.6 jit_solution(429413924595695594)
XLA Ops:
  0.6 0.0 copy-start
  0.6 0.0 copy-start.1
  0.6 92.9 %shard_map.41 = (f32[1,4096]{1,0:T(1,128)S(1)}, f32[1,4096]{1,0:T(1,128)S(1)}) custom-call(bf16[512,128]{1,0:T(8,128)(2,1)} %s_ref.1, bf16[256,128]{1,0:T(8,128)(2,1)} %t_ref.1), custom_call_target="tpu_custom_call" | custom-call | flops 25769803776 | bytes 2097152 | tf_op jit(solution)/shard_map/pallas_call | solution.py:653
  93.5 0.5 slice.3
  95.3 0.0 copy-done
  95.3 0.0 copy-done.1
  95.4 126.0 %conditional.1 = (f32[4096]{0:T(1024)S(1)}, f32[4096]{0:T(1024)S(1)}) conditional(s32[]{:T(128)} %bitcast.4, (f32[1,4096]{1,0:T(1,128)S(1)}, f32[1,4096]{1,0:T(1,128)S(1)}) %shard_map.41, (bf16[512,128]{1,0:T(8,128)(2,1)S(1)}, bf16[256,128]{1,0:T(8,128)(2,1)S(1)}) %tuple.29), branch_computations={%region_0.0_spmd, %region_1.0_spmd} | conditional | flops 25769803776 | bytes 2097168 | solution.py:696
  95.4 126.0 %branch_1_fun.1 = (f32[1,4096]{1,0:T(1,128)S(1)}, f32[1,4096]{1,0:T(1,128)S(1)}) custom-call(bf16[512,128]{1,0:T(8,128)(2,1)S(1)} %get-tuple-element.14.s_ref, bf16[256,128]{1,0:T(8,128)(2,1)S(1)} %get-tuple-element.15.t_ref), custom_call_target="tpu_custom_call" | custom-call | flops 25769803776 | bytes 2097152 | tf_op jit(solution)/shard_map/cond/branch_1_fun/pallas_call | solution.py:609
  221.4 0.6 copy.12
  222.0 0.6 copy.13
Async XLA Ops:
  0.6 94.7 %copy-start = (bf16[512,128]{1,0:T(8,128)(2,1)S(1)}, bf16[512,128]{1,0:T(8,128)(2,1)}, u32[]{:S(2)}) copy-start(bf16[512,128]{1,0:T(8,128)(2,1)} %s_ref.1) | copy-start | bytes 393220
  0.6 94.7 %copy-start.1 = (bf16[256,128]{1,0:T(8,128)(2,1)S(1)}, bf16[256,128]{1,0:T(8,128)(2,1)}, u32[]{:S(2)}) copy-start(bf16[256,128]{1,0:T(8,128)(2,1)} %t_ref.1) | copy-start | bytes 196612

commit v6 on v4

--- a/solution.py
+++ b/solution.py
@@ -42,9 +42,9 @@
 
 def kernel(
     row_n, col_n, s_ref, t_ref, f_ref, g_ref,
-    s_all, t_all, s_ext, t_ext, kept, sums, sums_t, highs, row_part, col_part, part, weight, s_sq, t_sq, shift_s, shift_t,
+    s_all, t_all, s_ext, t_ext, kept, sums, sums_t, highs, row_part, col_part, part, weight, s_sq, t_sq, shift_s, shift_t, sample, g_first,
     from_col, from_row,
-    s_send, s_recv, t_send, t_recv, pair_send, pair_recv, col_send, col_recv, row_send, row_recv,
+    s_send, s_recv, near_send, near_recv, far_send, far_recv, pair_send, pair_recv, col_send, col_recv, row_send, row_recv,
 ):
     own_s, depth = s_ref.shape
     own_t = t_ref.shape[0]
@@ -66,8 +66,27 @@
     def s_block(index):
         return pl.ds(pl.multiple_of(index * own_s, own_s), own_s)
 
-    def t_block(index):
-        return pl.ds(pl.multiple_of(index * own_t, own_t), own_t)
+    side = math.isqrt(row_n)
+    my_z, my_x = my_row // side, my_row % side
+    half_own = own_t // 2
+    chunk_t = side * half_own
+    chunks = 2 * side
+
+    def first_halves(z, x):
+        return pl.ds(pl.multiple_of((z * side + x) * half_own, half_own), half_own)
+
+    def second_halves(z, x):
+        return pl.ds(pl.multiple_of(nt // 2 + (x * side + z) * half_own, half_own), half_own)
+
+    def steps(p):
+        k = p // 2
+        return k + k // 2 - 2 * (k // 3)
+
+    def chunk_rows(p, sent=False):
+        second = p % 2
+        k = 0 if sent else steps(p)
+        line = (my_z * (1 - second) + my_x * second - k + side) % side
+        return pl.ds(pl.multiple_of(second * (nt // 2) + line * chunk_t, chunk_t), chunk_t)
 
     def s_from(k):
         return lax.rem(my_col - 2 * k + col_n, col_n)
@@ -75,13 +94,29 @@
     def twin_from(k):
         return lax.rem(twin - 2 * k + col_n, col_n)
 
-    def t_from(k):
-        return lax.rem(my_row - k + row_n, row_n)
-
-    def t_copy(k):
+    def near_copies():
+        copies = []
+        for k in range(1, side):
+            for second in range(2):
+                z = (my_z + k * second) % side
+                x = (my_x + k * (1 - second)) % side
+                here = t_ref.at[pl.ds(second * half_own, half_own), :]
+                there = t_all.at[second_halves(my_z, my_x) if second else first_halves(my_z, my_x), :]
+                copies.append(
+                    pltpu.make_async_remote_copy(
+                        here, there, near_send.at[second, k], near_recv.at[second, k],
+                        device_id={"row": z * side + x}, device_id_type=MESH,
+                    )
+                )
+        return copies
+
+    def chunk_copy(p):
+        second = p % 2
+        at = t_all.at[chunk_rows(p, True), :]
+        z = (my_z + steps(p) * (1 - second)) % side
+        x = (my_x + steps(p) * second) % side
         return pltpu.make_async_remote_copy(
-            t_ref, t_all.at[t_block(my_row), :], t_send.at[k], t_recv.at[k],
-            device_id={"row": lax.rem(my_row + k, row_n)}, device_id_type=MESH,
+            at, at, far_send.at[p], far_recv.at[p], device_id={"row": z * side + x}, device_id_type=MESH
         )
 
     def s_copy(k):
@@ -97,11 +132,11 @@
         )
 
     pl.semaphore_wait(barrier, col_n + row_n - 2)
+    for copy in near_copies():
+        copy.start()
     for k in range(1, chips):
         s_copy(k).start()
     twin_copy(0).start()
-    for k in range(1, row_n):
-        t_copy(k).start()
 
     chunk = 128
 
@@ -116,27 +151,34 @@
         select = ones_at(16, first)[1].astype(BF16)
         return nt_dot(select, ext)[0:1, :]
 
-    def t_prepare(index):
-        lane, ones = ones_at(own_t, 3)
-        for i in index:
-            x = t_all[t_block(i), :].astype(F32)
-            bias = spread(jnp.sum(x * x, axis=1, keepdims=True) * -0.5)
-            t_ext[t_block(i), :] = pick3(bias, lane, 0, ones)
+    def bias_beside(x):
+        x = x.astype(F32)
+        lane, ones = ones_at(x.shape[0], 3)
+        return pick3(spread(jnp.sum(x * x, axis=1, keepdims=True) * -0.5), lane, 0, ones)
+
+    def t_prepare(p):
+        t_ext[chunk_rows(p), :] = bias_beside(t_all[chunk_rows(p), :])
 
     def s_prepare(i):
         lane, ones = ones_at(own_s, 0)
-        sample = jnp.concatenate([t_ref[...], t_ext[t_block(my_row), :]], axis=1)
         x = jnp.concatenate([s_all[s_block(i), :], ones.astype(BF16)], axis=1)
-        shift = spread(-FLOOR / SCALE - jnp.max(nt_dot(x, sample), axis=1, keepdims=True))
+        shift = spread(-FLOOR / SCALE - jnp.max(nt_dot(x, sample[...]), axis=1, keepdims=True))
         s_ext[s_block(i), :] = pick3(shift, lane, 3, ones)
 
     s_all[s_block(my_col), :] = s_ref[...]
-    t_all[t_block(my_row), :] = t_ref[...]
+    t_all[first_halves(my_z, my_x), :] = t_ref[0:half_own, :]
+    t_all[second_halves(my_z, my_x), :] = t_ref[half_own:own_t, :]
+    sample[...] = jnp.concatenate([t_ref[...], bias_beside(t_ref[...])], axis=1)
     sums[...] = jnp.zeros_like(sums)
-    t_prepare([my_row])
+    highs[...] = jnp.full_like(highs, -3e38)
     s_prepare(my_col)
-
-    per = 2
+    for copy in near_copies():
+        copy.wait()
+    for p in range(2, chunks):
+        chunk_copy(p).start()
+    for p in range(2):
+        t_prepare(p)
+
     half_s, half_t = ns // 2, nt // 2
     halves = (0, 1)
 
@@ -146,22 +188,17 @@
     def t_half(h):
         return pl.ds(h * half_t, half_t)
 
-    def terms_with(t_index, h):
-        x = jnp.concatenate(
-            [jnp.concatenate([t_all[t_block(i), :], t_ext[t_block(i), :]], axis=1) for i in t_index], axis=0
-        )
-        high = None
+    def terms_with(p, h):
+        x = jnp.concatenate([t_all[chunk_rows(p), :], t_ext[chunk_rows(p), :]], axis=1)
+        high = highs[chunk_rows(p), :]
         for i in range(h * col_n // 2, (h + 1) * col_n // 2):
             at = pl.ds(i * own_s, own_s)
             z = nt_dot(x, jnp.concatenate([s_all[at, :], s_ext[at, :]], axis=1))
             for c in range(0, own_s, depth):
-                piece = z[:, c : c + depth]
-                high = piece if high is None else jnp.maximum(high, piece)
-            terms = jnp.exp2(z * SCALE).reshape(z.shape[0] // 8, 8, own_s)
+                high = jnp.maximum(high, z[:, c : c + depth])
+            terms = jnp.exp2(z * SCALE).reshape(chunk_t // 8, 8, own_s)
             sums[:, at] = sums[:, at] + jnp.sum(terms, axis=0)
-        for n, i in enumerate(t_index):
-            at = t_block(i)
-            highs[at, :] = jnp.maximum(highs[at, :], high[n * own_t : (n + 1) * own_t, :])
+        highs[chunk_rows(p), :] = high
 
     def over(axis, turn, h):
         if axis == "col":
@@ -203,41 +240,35 @@
         s_copy(k).wait_recv()
         twin_copy(k).start()
         s_prepare(s_from(k))
-    for j in range(1, per):
-        t_copy(j).wait_recv()
-    t_prepare([t_from(j) for j in range(1, per)])
-    highs[...] = jnp.full_like(highs, -3e38)
     for k in range(chips):
         twin_copy(k).wait_recv()
         s_prepare(twin_from(k))
 
     def early(p, _):
-        terms_with([t_from(per * p + j) for j in range(per)], 0)
-
-        @pl.when(p < row_n // per - 1)
+        terms_with(p, 0)
+
+        @pl.when((p > 0) & (p < chunks - 1))
         def _():
-            following = [per * p + per + j for j in range(per)]
-            for k in following:
-                t_copy(k).wait_recv()
-            t_prepare([t_from(k) for k in following])
+            chunk_copy(p + 1).wait_recv()
+            t_prepare(p + 1)
 
         return 0
 
     def late(p, _):
-        terms_with([t_from(per * p + j) for j in range(per)], 1)
+        terms_with(p, 1)
         return 0
 
-    lax.fori_loop(0, row_n // per, early, 0)
+    lax.fori_loop(0, chunks, early, 0)
     send_logs(0)
-    lax.fori_loop(0, row_n // per, late, 0)
+    lax.fori_loop(0, chunks, late, 0)
     send_logs(1)
 
     for k in range(1, chips):
         s_copy(k).wait_send()
     for k in range(chips):
         twin_copy(k).wait_send()
-    for k in range(1, row_n):
-        t_copy(k).wait_send()
+    for p in range(2, chunks):
+        chunk_copy(p).wait_send()
 
     room = (FLOOR + math.log2(total_t) - CEIL) / SCALE
 
@@ -343,15 +374,19 @@
             if turn == 1:
                 logs = combined_logs(arrived)
                 held = logs + shift_t[:, at] * SCALE
-                g_ref[:, at] = jnp.where(held > -30.0, math.log2(total_s) - logs, jnp.nan)
-                weight[0, :, at] = jnp.exp2(g_ref[:, at] - shift_t[:, at] * SCALE)
+                g_first[:, at] = jnp.where(held > -30.0, math.log2(total_s) - logs, jnp.nan)
+                weight[0, :, at] = jnp.exp2(g_first[:, at] - shift_t[:, at] * SCALE)
                 weight[1, :, at] = weight[0, :, at]
             else:
                 v = total_s / sum(arrived)
                 if turn < ITERS:
                     weight[1, :, at] = weight[0, :, at] * v
                 else:
-                    g_ref[:, at] = BACK * (g_ref[:, at] + log2(v)) + t_sq[:, at]
+                    found = BACK * (g_first[:, at] + log2(v)) + t_sq[:, at]
+                    for i in range(row_n):
+                        z, x = (i % side, i // side) if h else (i // side, i % side)
+                        begin = (z * side + x) * own_t + h * half_own
+                        g_ref[:, begin : begin + half_own] = found[:, i * half_own : (i + 1) * half_own]
             if turn < ITERS and h == 0:
                 lax.fori_loop(0, ns // size, row_sums(0, None), 0)
         if turn == ITERS:
@@ -652,12 +687,16 @@
             pltpu.VMEM((1, nt), F32),
             pltpu.VMEM((1, ns), F32),
             pltpu.VMEM((1, nt), F32),
+            pltpu.VMEM((own_t, 2 * depth), BF16),
+            pltpu.VMEM((1, nt), F32),
             pltpu.VMEM((ITERS, col_n - 1, 1, ns), F32),
             pltpu.VMEM((ITERS, row_n - 1, 1, nt), F32),
             dma((col_n // 2,)),
             dma((col_n // 2,)),
-            dma((row_n,)),
-            dma((row_n,)),
+            dma((2, math.isqrt(row_n))),
+            dma((2, math.isqrt(row_n))),
+            dma((2 * math.isqrt(row_n),)),
+            dma((2 * math.isqrt(row_n),)),
             dma((col_n // 2,)),
             dma((col_n // 2,)),
             dma((ITERS, 2, col_n - 1)),

time: 221 us -> 221 us (level)
  no operation moved by 1% of the time
where the time goes in v6:
time: 221 us; the launch traced here: 220 us
  Pallas kernels  216 us (98%)
    pallas_call x1, Pallas kernels, careful(): pl.pallas_call(functools.partial(careful_kernel, row_n, col_n), out_shape...  126 us
    pallas_call x1, Pallas kernels, on_device(): pl.pallas_call(functools.partial(kernel, row_n, col_n), out_shape=(jax.Sh...  90.6 us

profile of v6, /device:TPU:0, one launch (start us, length us, event | category | flops | bytes accessed | tf_op | source)
XLA Modules:
  0.0 220.1 jit_solution(8928093149328510843)
XLA Ops:
  0.6 0.0 copy-start
  0.6 0.0 copy-start.1
  0.6 90.6 %shard_map.41 = (f32[1,4096]{1,0:T(1,128)S(1)}, f32[1,4096]{1,0:T(1,128)S(1)}) custom-call(bf16[512,128]{1,0:T(8,128)(2,1)} %s_ref.1, bf16[256,128]{1,0:T(8,128)(2,1)} %t_ref.1), custom_call_target="tpu_custom_call" | custom-call | flops 25769803776 | bytes 2097152 | tf_op jit(solution)/shard_map/pallas_call | solution.py:668
  91.3 0.5 slice.3
  93.1 0.0 copy-done
  93.1 0.0 copy-done.1
  93.1 125.8 %conditional.1 = (f32[4096]{0:T(1024)S(1)}, f32[4096]{0:T(1024)S(1)}) conditional(s32[]{:T(128)} %bitcast.4, (f32[1,4096]{1,0:T(1,128)S(1)}, f32[1,4096]{1,0:T(1,128)S(1)}) %shard_map.41, (bf16[512,128]{1,0:T(8,128)(2,1)S(1)}, bf16[256,128]{1,0:T(8,128)(2,1)S(1)}) %tuple.29), branch_computations={%region_0.0_spmd, %region_1.0_spmd} | conditional | flops 25769803776 | bytes 2097168 | solution.py:715
  93.1 125.8 %branch_1_fun.1 = (f32[1,4096]{1,0:T(1,128)S(1)}, f32[1,4096]{1,0:T(1,128)S(1)}) custom-call(bf16[512,128]{1,0:T(8,128)(2,1)S(1)} %get-tuple-element.14.s_ref, bf16[256,128]{1,0:T(8,128)(2,1)S(1)} %get-tuple-element.15.t_ref), custom_call_target="tpu_custom_call" | custom-call | flops 25769803776 | bytes 2097152 | tf_op jit(solution)/shard_map/cond/branch_1_fun/pallas_call | solution.py:624
  218.9 0.6 copy.12
  219.5 0.6 copy.13
Async XLA Ops:
  0.6 92.5 %copy-start = (bf16[512,128]{1,0:T(8,128)(2,1)S(1)}, bf16[512,128]{1,0:T(8,128)(2,1)}, u32[]{:S(2)}) copy-start(bf16[512,128]{1,0:T(8,128)(2,1)} %s_ref.1) | copy-start | bytes 393220
  0.6 92.5 %copy-start.1 = (bf16[256,128]{1,0:T(8,128)(2,1)S(1)}, bf16[256,128]{1,0:T(8,128)(2,1)}, u32[]{:S(2)}) copy-start(bf16[256,128]{1,0:T(8,128)(2,1)} %t_ref.1) | copy-start | bytes 196612

commit v7 on v6

--- a/solution.py
+++ b/solution.py
@@ -42,7 +42,7 @@
 
 def kernel(
     row_n, col_n, s_ref, t_ref, f_ref, g_ref,
-    s_all, t_all, s_ext, t_ext, kept, sums, sums_t, highs, row_part, col_part, part, weight, s_sq, t_sq, shift_s, shift_t, sample, g_first,
+    s_all, t_all, s_ext, t_ext, kept, sums, sums_t, highs, row_part, col_part, part, weight, s_sq, t_sq, shift_s, shift_t, sample, g_first, weight_low,
     from_col, from_row,
     s_send, s_recv, near_send, near_recv, far_send, far_recv, pair_send, pair_recv, col_send, col_recv, row_send, row_recv,
 ):
@@ -339,6 +339,9 @@
     size = min(512, half_s)
     fine = min(64, size)
 
+    def set_weight(at, x):
+        weight_low[:, at] = jnp.broadcast_to(x, (16, half_t)).astype(BF16)
+
     def row_sums(h, out):
         def one(i, _):
             for q in range(0, size, 128):
@@ -346,8 +349,13 @@
                 for r in range(q, q + 128, fine):
                     rows = pl.ds(pl.multiple_of(i * size, size) + r, fine)
                     summed = jnp.zeros((fine, 128), F32) if out is None else row_part[rows, :]
-                    for c in range(h * half_t, (h + 1) * half_t, 128):
-                        summed = summed + kept[rows, c : c + 128].astype(F32) * weight[1, :, c : c + 128]
+                    for c in range(h * half_t, (h + 1) * half_t, 512):
+                        terms = [
+                            kept[rows, d : d + 128] * jnp.tile(weight_low[:, d : d + 128], (fine // 16, 1))
+                            for d in range(c, c + 512, 128)
+                            if d < (h + 1) * half_t
+                        ]
+                        summed = summed + functools.reduce(jnp.add, terms).astype(F32)
                     if out is None:
                         row_part[rows, :] = summed
                     pieces.append(summed)
@@ -376,11 +384,11 @@
                 held = logs + shift_t[:, at] * SCALE
                 g_first[:, at] = jnp.where(held > -30.0, math.log2(total_s) - logs, jnp.nan)
                 weight[0, :, at] = jnp.exp2(g_first[:, at] - shift_t[:, at] * SCALE)
-                weight[1, :, at] = weight[0, :, at]
+                set_weight(at, weight[0, :, at])
             else:
                 v = total_s / sum(arrived)
                 if turn < ITERS:
-                    weight[1, :, at] = weight[0, :, at] * v
+                    set_weight(at, weight[0, :, at] * v)
                 else:
                     found = BACK * (g_first[:, at] + log2(v)) + t_sq[:, at]
                     for i in range(row_n):
@@ -682,13 +690,14 @@
             pltpu.VMEM((ns, 128), F32),
             pltpu.VMEM((1, nt), F32),
             pltpu.VMEM((2 * ITERS, 1, max(ns, nt)), F32),
-            pltpu.VMEM((2, 1, nt), F32),
+            pltpu.VMEM((1, 1, nt), F32),
             pltpu.VMEM((1, ns), F32),
             pltpu.VMEM((1, nt), F32),
             pltpu.VMEM((1, ns), F32),
             pltpu.VMEM((1, nt), F32),
             pltpu.VMEM((own_t, 2 * depth), BF16),
             pltpu.VMEM((1, nt), F32),
+            pltpu.VMEM((16, nt), BF16),
             pltpu.VMEM((ITERS, col_n - 1, 1, ns), F32),
             pltpu.VMEM((ITERS, row_n - 1, 1, nt), F32),
             dma((col_n // 2,)),

time: 221 us -> 219 us (level)
  no operation moved by 1% of the time
where the time goes in v7:
time: 219 us
  Pallas kernels  215 us (98%)
    pallas_call x1, Pallas kernels, careful(): pl.pallas_call(functools.partial(careful_kernel, row_n, col_n), out_shape...  126 us
    pallas_call x1, Pallas kernels, on_device(): pl.pallas_call(functools.partial(kernel, row_n, col_n), out_shape=(jax.Sh...  88.4 us

profile of v7, /device:TPU:0, one launch (start us, length us, event | category | flops | bytes accessed | tf_op | source)
XLA Modules:
  0.0 218.7 jit_solution(13214434440410380423)
XLA Ops:
  0.6 0.0 copy-start
  0.6 0.0 copy-start.1
  0.6 88.4 %shard_map.41 = (f32[1,4096]{1,0:T(1,128)S(1)}, f32[1,4096]{1,0:T(1,128)S(1)}) custom-call(bf16[512,128]{1,0:T(8,128)(2,1)} %s_ref.1, bf16[256,128]{1,0:T(8,128)(2,1)} %t_ref.1), custom_call_target="tpu_custom_call" | custom-call | flops 25769803776 | bytes 2097152 | tf_op jit(solution)/shard_map/pallas_call | solution.py:676
  89.1 0.5 slice.3
  90.9 0.0 copy-done
  90.9 0.0 copy-done.1
  90.9 126.5 %conditional.1 = (f32[4096]{0:T(1024)S(1)}, f32[4096]{0:T(1024)S(1)}) conditional(s32[]{:T(128)} %bitcast.4, (f32[1,4096]{1,0:T(1,128)S(1)}, f32[1,4096]{1,0:T(1,128)S(1)}) %shard_map.41, (bf16[512,128]{1,0:T(8,128)(2,1)S(1)}, bf16[256,128]{1,0:T(8,128)(2,1)S(1)}) %tuple.29), branch_computations={%region_0.0_spmd, %region_1.0_spmd} | conditional | flops 25769803776 | bytes 2097168 | solution.py:724
  90.9 126.5 %branch_1_fun.1 = (f32[1,4096]{1,0:T(1,128)S(1)}, f32[1,4096]{1,0:T(1,128)S(1)}) custom-call(bf16[512,128]{1,0:T(8,128)(2,1)S(1)} %get-tuple-element.14.s_ref, bf16[256,128]{1,0:T(8,128)(2,1)S(1)} %get-tuple-element.15.t_ref), custom_call_target="tpu_custom_call" | custom-call | flops 25769803776 | bytes 2097152 | tf_op jit(solution)/shard_map/cond/branch_1_fun/pallas_call | solution.py:632
  217.4 0.6 copy.12
  218.0 0.6 copy.13
Async XLA Ops:
  0.6 90.3 %copy-start = (bf16[512,128]{1,0:T(8,128)(2,1)S(1)}, bf16[512,128]{1,0:T(8,128)(2,1)}, u32[]{:S(2)}) copy-start(bf16[512,128]{1,0:T(8,128)(2,1)} %s_ref.1) | copy-start | bytes 393220
  0.6 90.3 %copy-start.1 = (bf16[256,128]{1,0:T(8,128)(2,1)S(1)}, bf16[256,128]{1,0:T(8,128)(2,1)}, u32[]{:S(2)}) copy-start(bf16[256,128]{1,0:T(8,128)(2,1)} %t_ref.1) | copy-start | bytes 196612
